TPU v7x, 128 devices: a whole 4x4x4 slice. The times are simulated.
128 devices in a mesh: seq: 32 (over x, z, core), head: 4 (over y).
Axes of the slice: x: 4, y: 4, z: 4, core: 2. Of those that a mesh axis runs over, the one named last changes fastest.
Arguments:
- queries: bfloat16 [24576, 8192], P('seq', 'head'), may hold values from -3 to 3
- keys: bfloat16 [24576, 8192], P('seq', 'head'), may hold values from -3 to 3
- values: bfloat16 [24576, 8192], P('seq', 'head'), may hold values from -13 to 13
- log_decay: float32 [64, 24576], P('head', 'seq'), may hold values from -1 to 0, as said below
- gain: float32 [8192], P('head'), may hold values from 0.25 to 1.75
- grad_out: bfloat16 [24576, 8192], P('seq', 'head'), may hold values from -5 to 5
Outputs:
- output: bfloat16 [24576, 8192], P('seq', 'head')
- grad_queries: bfloat16 [24576, 8192], P('seq', 'head')
- grad_keys: bfloat16 [24576, 8192], P('seq', 'head')
- grad_values: bfloat16 [24576, 8192], P('seq', 'head')
- grad_gain: float32 [8192], P('head')
Inputs may be any that keep to these rules, and one draw needn't show every extreme that they name: `log_decay`: every entry is negative.
All inputs are finite; a program needn't handle non-finite values.
Results may differ from a plain program's by a relative error of at most 0.012.
Values sent between devices are 32-bit elements; how exact they have to be, the bound alone decides.
No kernel may reach another device: no remote copies, remote signals or barrier semaphores. Data moves between devices by JAX's collectives and lax.ppermute only.
A program may use at most 192 MiB of HBM per device.

v0:
```python
import functools

import jax
import jax.numpy as jnp
from jax import lax
from jax.experimental import pallas as pl
from jax.experimental.pallas import tpu as pltpu
from jax.sharding import PartitionSpec as P

HEAD_TOTAL = 64
DH = 128
SPAN = 128
ROWS = 8
STATES = 2 * DH
PIECE = STATES + ROWS
GROUP = 4
PAIR = 2
ALONG_X, ALONG_Z = 4, 4
F32 = jnp.float32
BF16 = jnp.bfloat16
EXACT = lax.Precision.HIGHEST
VMEM = pl.BlockSpec(memory_space=pltpu.VMEM)
HBM = pl.BlockSpec(memory_space=pltpu.HBM)
ANY = pl.BlockSpec(memory_space=pl.ANY)


def dot(a, b, contract, precision=None):
    return lax.dot_general(
        a, b, ((contract[:1], contract[1:]), ((), ())), precision=precision, preferred_element_type=F32
    )


def nn(a, b):
    return dot(a, b, (1, 0))


def nt(a, b):
    return dot(a, b, (1, 1))


def params(mib):
    return pltpu.CompilerParams(vmem_limit_bytes=mib * 1024 * 1024)


def cost(flops, nbytes):
    return pl.CostEstimate(flops=int(flops), bytes_accessed=int(nbytes), transcendentals=0)


def head_rows(ref, head):
    return ref[pl.ds(pl.multiple_of(head * ROWS, ROWS), ROWS), :]


def head_lanes(head, count=1):
    return pl.ds(pl.multiple_of(head * DH, DH), count * DH)


def span(n):
    return slice(n * SPAN, (n + 1) * SPAN)


def last_lane(rows):
    return jnp.broadcast_to(rows[:, SPAN - 1 :], rows.shape)


def middle_lane(rows):
    return jnp.broadcast_to(rows[:, SPAN // 2 - 1 : SPAN // 2], rows.shape)


def masks():
    i = lax.broadcasted_iota(jnp.int32, (SPAN, SPAN), 0)
    j = lax.broadcasted_iota(jnp.int32, (SPAN, SPAN), 1)
    return i >= j, i <= j


def join_rows(rows, blocks):
    return jnp.concatenate([rows[n : n + 1] for n in range(blocks)], axis=1)


def piece_store(ref, at, state, extra):
    pair, which = divmod(at, 2)
    ref[pair, which * DH : (which + 1) * DH, :] = state
    ref[pair, STATES + 4 * which : STATES + 4 * which + 4, :] = extra[:4]


def piece_state(ref, at):
    pair, which = divmod(at, 2)
    return ref[pair, which * DH : (which + 1) * DH, :]


def each_state(piece):
    return [(slice(w * DH, (w + 1) * DH), slice(STATES + 4 * w, STATES + 4 * w + 1)) for w in range(2)]


def extra_rows(decay, gain_row=None):
    place = lax.broadcasted_iota(jnp.int32, (ROWS, DH), 0)
    rest = 0.0 if gain_row is None else jnp.where(place == 1, gain_row, 0.0)
    return jnp.where(place == 0, decay, rest)


def position():
    place = lax.axis_index("seq")
    return lax.rem(place, 2), lax.rem(place // 2, ALONG_Z), place // (2 * ALONG_Z)


def half_heads(core, of_other, at, heads):
    half = heads // 2
    start = (1 - core) if of_other else core
    return start * half + at


def decay_tables(log_ref, cum_ref, before_ref, total_ref):
    heads, rows = log_ref.shape
    _, triangle = masks()
    triangle = triangle.astype(F32)
    cum_ref[...] = jnp.zeros_like(cum_ref)
    before_ref[...] = jnp.zeros_like(before_ref)
    before = jnp.zeros((heads, SPAN), F32)
    for n in range(rows // SPAN):
        cum = dot(log_ref[:, span(n)], triangle, (1, 0), EXACT)
        for h in range(heads):
            cum_ref[h * ROWS + n : h * ROWS + n + 1, :] = cum[h : h + 1]
            before_ref[h * ROWS + n : h * ROWS + n + 1, :] = before[h : h + 1]
        before = before + last_lane(cum)
    for h in range(heads):
        total_ref[h * ROWS : (h + 1) * ROWS, :] = jnp.broadcast_to(before[h : h + 1], (ROWS, SPAN))


def state_body(of_other, *refs):
    core, _, _ = position()
    if of_other:
        k_hbm, v_hbm, log_hbm, out_ref, k_ref, v_ref, cum_ref, before_ref, total_ref, sems, log_ref, log_sem = refs
    else:
        k_ref, v_ref, cum_ref, before_ref, total_ref, out_ref = refs
    rows, width = k_ref.shape
    heads, blocks = width // DH, rows // SPAN
    copies = []
    if of_other:
        log_copy = pltpu.make_async_copy(log_hbm, log_ref, log_sem)
        log_copy.start()
        for g in range(heads // GROUP):
            lanes = head_lanes(lax.rem(half_heads(core, True, g * GROUP, heads), heads), GROUP)
            for which, (source, target) in enumerate(((k_hbm, k_ref), (v_hbm, v_ref))):
                copies.append(pltpu.make_async_copy(source.at[:, lanes], target.at[:, lanes], sems.at[which, g]))
                copies[-1].start()
        log_copy.wait()
        decay_tables(log_ref, cum_ref, before_ref, total_ref)

    for g in range(heads // 2 // GROUP):
        first = half_heads(core, of_other, g * GROUP, heads)
        if of_other:
            copies[2 * g].wait()
            copies[2 * g + 1].wait()
        totals = [head_rows(total_ref, first + at) for at in range(GROUP)]
        scales = [
            jnp.exp(totals[at] - head_rows(before_ref, first + at) - head_rows(cum_ref, first + at)) for at in range(GROUP)
        ]
        decayed = [
            (k_ref[:, head_lanes(first + at)].T.astype(F32) * join_rows(scales[at], blocks)).astype(BF16)
            for at in range(GROUP)
        ]
        states = [nn(decayed[at], v_ref[:, head_lanes(first + at)]) for at in range(GROUP)]
        for at in range(GROUP):
            piece_store(out_ref, g * GROUP + at, states[at], extra_rows(jnp.exp(totals[at])))
    for copy in copies[heads // GROUP :]:
        copy.wait()


def local_state(of_other, keys, values, more):
    rows, width = keys.shape
    heads = width // DH
    pieces = jax.ShapeDtypeStruct((heads // 4, PIECE, DH), F32)
    table = jax.ShapeDtypeStruct((heads * ROWS, SPAN), F32)
    like = jax.ShapeDtypeStruct(keys.shape, BF16)
    if of_other:
        specs, outs = [HBM] * 3, [pieces, like, like, table, table, table]
        scratch = [
            pltpu.SemaphoreType.DMA((2, heads // GROUP)),
            pltpu.VMEM(more[0].shape, F32),
            pltpu.SemaphoreType.DMA,
        ]
    else:
        specs, outs, scratch = [VMEM] * 5, [pieces], []
    return pl.pallas_call(
        functools.partial(state_body, of_other),
        in_specs=specs,
        out_specs=[VMEM] * len(outs),
        out_shape=outs,
        scratch_shapes=scratch,
        compiler_params=params(4),
        cost_estimate=cost(heads * rows * DH * DH, 2 * rows * heads * DH),
        name="state_given" if of_other else "state_kept",
    )(keys, values, *more)


def arrival_order(count):
    return [0] + sorted(range(1, count), key=lambda s: -min(s, count - s))


def join_extra(a, b):
    decays = lax.broadcasted_iota(jnp.int32, (ROWS, DH), 0) % 4 == 0
    return jnp.where(decays, a * b, a + b)


def cores_body(reverse, own_ref, got_ref, *out_refs):
    core, z, _ = position()
    near_here = (core == 0) != reverse
    for shift, out_ref in enumerate(out_refs):
        pair = lax.rem(z + shift, ALONG_Z)
        own, got = own_ref[pair], got_ref[pair]
        near, far = jnp.where(near_here, own, got), jnp.where(near_here, got, own)
        for rows, decay in each_state(near):
            out_ref[rows, :] = far[decay] * near[rows] + far[rows]
        out_ref[STATES:, :] = join_extra(near[STATES:], far[STATES:])


def along_z_body(reverse, *refs):
    in_refs, (_, total_ref, prefix_ref, slots) = refs[:ALONG_Z], refs[ALONG_Z:]
    _, z, _ = position()
    for shift, ref in zip(arrival_order(len(in_refs)), in_refs):
        slots[lax.rem(z - shift + ALONG_Z, ALONG_Z)] = ref[...]
    laps = [ALONG_Z - 1 - lap if reverse else lap for lap in range(ALONG_Z)]
    for rows, decay in each_state(total_ref):
        state = jnp.zeros((DH, DH), F32)
        for at in laps:
            prefix_ref[at, rows, :] = state
            state = slots[at, decay, :] * state + slots[at, rows, :]
        total_ref[rows, :] = state
    extra = jnp.where(lax.broadcasted_iota(jnp.int32, (ROWS, DH), 0) % 4 == 0, 1.0, 0.0)
    for at in laps:
        prefix_ref[at, STATES:, :] = extra
        extra = join_extra(extra, slots[at, STATES:, :])
    total_ref[STATES:, :] = extra


def along_x_body(reverse, *refs):
    in_refs, prefix_ref, out_refs, slots = refs[:ALONG_X], refs[ALONG_X], refs[ALONG_X + 2 : -1], refs[-1]
    _, z, x = position()
    for shift, ref in zip(arrival_order(len(in_refs)), in_refs):
        slots[lax.rem(x - shift + ALONG_X, ALONG_X)] = ref[...]
    for rows, decay in each_state(prefix_ref):
        state = jnp.zeros((DH, DH), F32)
        for lap in range(ALONG_X):
            at = ALONG_X - 1 - lap if reverse else lap
            taken = (at > x) if reverse else (at < x)
            state = jnp.where(taken, slots[at, decay, :] * state + slots[at, rows, :], state)
        for shift, out_ref in enumerate(out_refs):
            at = lax.rem(z + shift, ALONG_Z)
            out_ref[rows, :] = prefix_ref[at, rows, :] + prefix_ref[at, decay, :] * state
    if reverse:
        extra = sum(slots[at, STATES:, :] for at in range(ALONG_X))
        for out_ref in out_refs:
            out_ref[STATES:, :] = extra


def entering_body(reverse, *refs):
    in_refs, (own_ref, got_ref, _, keep_ref, give_ref) = refs[:ALONG_Z], refs[ALONG_Z:]
    core, z, _ = position()
    near_here = (core == 0) != reverse
    for shift, ref in zip(arrival_order(len(in_refs)), in_refs):
        pair = lax.rem(z - shift + ALONG_Z, ALONG_Z)
        near = jnp.where(near_here, own_ref[pair], got_ref[pair])
        for rows, decay in each_state(near):
            entering = ref[rows, :]
            passed = near[decay] * entering + near[rows]
            keep_ref[pair, rows, :] = jnp.where(near_here, entering, passed)
            give_ref[pair, rows, :] = jnp.where(near_here, passed, entering)
        if reverse:
            keep_ref[pair, STATES:, :] = ref[STATES:, :]
            give_ref[pair, STATES:, :] = ref[STATES:, :]


def scan_step(body, name, reverse, arrays, after, out_counts, scratch):
    shapes = [jax.ShapeDtypeStruct(shape, F32) for shape in out_counts]
    afters = [] if after is None else [after]
    return pl.pallas_call(
        functools.partial(body, reverse),
        in_specs=[VMEM] * len(arrays) + [ANY] * len(afters),
        out_specs=[VMEM] * len(shapes),
        out_shape=shapes,
        scratch_shapes=scratch,
        compiler_params=params(3),
        cost_estimate=cost(10**6, 10**6),
        name=name,
    )(*arrays, *afters)


def scan_over_seq(send, own, reverse, works):
    count = lax.axis_size("seq")

    def index(x, z, c):
        return (x % ALONG_X * ALONG_Z + z % ALONG_Z) * 2 + c

    every = [(x, z, c) for x in range(ALONG_X) for z in range(ALONG_Z) for c in range(2)]
    across = [(i, i ^ 1) for i in range(count)]
    by_z = [[(index(x, z, c), index(x, z + s, c)) for x, z, c in every] for s in range(ALONG_Z)]
    by_x = [[(index(x, z, c), index(x + s, z, c)) for x, z, c in every] for s in range(ALONG_X)]
    piece = (PIECE, DH)
    back = (PIECE if reverse else STATES, DH)

    def shifted(arrays, moves):
        return [lax.ppermute(arrays[s], "seq", moves[s]) if s else arrays[0] for s in arrival_order(len(moves))]

    got = lax.ppermute(send, "seq", across)
    parts = scan_step(cores_body, "join_cores", reverse, [own, got], None, [piece] * ALONG_Z, [])
    arrived = shifted(parts, by_z)
    done = works[0](parts[0], ())
    total, prefix = scan_step(
        along_z_body, "join_z", reverse, arrived, done[-1],
        [piece, (ALONG_Z,) + piece], [pltpu.VMEM((ALONG_Z,) + piece, F32)],
    )
    totals = shifted([total] * ALONG_X, by_x)
    done = works[1](total, done)
    parts = scan_step(
        along_x_body, "join_x", reverse, totals + [prefix], done[-1],
        [back] * ALONG_Z, [pltpu.VMEM((ALONG_X,) + piece, F32)],
    )
    arrived = shifted(parts, by_z)
    done = works[2](parts[0], done)
    keep, give = scan_step(
        entering_body, "entering", reverse, arrived + [own, got], done[-1], [own.shape[:1] + back] * 2, []
    )
    return keep, lax.ppermute(give, "seq", across), done


def block_picks(blocks):
    part = lax.broadcasted_iota(jnp.int32, (4 * ROWS, blocks * SPAN), 0)
    place = lax.broadcasted_iota(jnp.int32, (4 * ROWS, blocks * SPAN), 1)
    return (lax.rem(part, ROWS) == place // SPAN).astype(BF16)


def spread(rows, picks):
    high = rows.astype(BF16).astype(F32)
    middle = (rows - high).astype(BF16).astype(F32)
    parts = jnp.concatenate([high, middle, rows - high - middle, jnp.zeros_like(rows)], axis=0)
    return nn(parts.T.astype(BF16), picks)


def staggered(stages, steps):
    for at in range(len(steps) + len(stages) - 1):
        for back, stage in enumerate(stages):
            if 0 <= at - back < len(steps):
                stage(*steps[at - back])


def attend_heads(heads, q_ref, k_ref, v_ref, cum_ref, outs, both_masks, picks):
    local_ref, low_ref, turned_ref, qs_ref, ks_ref, vs_ref, weights_ref = outs
    mask, turned_mask = both_masks
    blocks = k_ref.shape[0] // SPAN
    each = range(len(heads))
    steps = [(a, n) for n in range(blocks) for a in each]
    lanes = [head_lanes(h) for h in heads]
    cums = [head_rows(cum_ref, h) for h in heads]
    mids = [middle_lane(c) for c in cums]
    ends = [last_lane(c) for c in cums]
    shifts = [spread(c - m, picks) for c, m in zip(cums, mids)]
    mid_scale, end_scale = [jnp.exp(m) for m in mids], [jnp.exp(e) for e in ends]
    rest_scale = [jnp.exp(e - m) for e, m in zip(ends, mids)]
    q_up, k_up, q_turned, k_turned, scores, turned_weights, updates, weights, lows, totals = ({} for _ in range(10))
    state = {a: jnp.zeros((DH, DH), F32) for a in each}

    def scale(a, n):
        shift = shifts[a][:, span(n)]
        up, down = jnp.exp(shift), jnp.exp(-shift)
        q_up[a, n] = (q_ref[span(n), lanes[a]].astype(F32) * up).astype(BF16)
        k_up[a, n] = (k_ref[span(n), lanes[a]].astype(F32) * down).astype(BF16)
        vs_ref[span(n), lanes[a]] = (v_ref[span(n), lanes[a]].astype(F32) * down).astype(BF16)
        qs_ref[span(n), lanes[a]] = q_up[a, n]
        ks_ref[span(n), lanes[a]] = k_up[a, n]

    def turn(a, n):
        k_turned[a, n] = k_up[a, n].T
        q_turned[a, n] = q_up[a, n].T
        turned_ref[heads[a], :, span(n)] = q_turned[a, n]

    def multiply(a, n):
        scores[a, n] = nn(q_up[a, n], k_turned[a, n])
        turned_weights[a, n] = nn(k_up[a, n], q_turned[a, n])
        if n < blocks - 1:
            updates[a, n] = nn(k_turned[a, n], v_ref[span(n), lanes[a]])

    def mask_out(a, n):
        weights[a, n] = jnp.where(mask, scores[a, n], 0.0).astype(BF16)
        weights_ref[heads[a], n] = jnp.where(turned_mask, turned_weights[a, n], 0.0).astype(BF16)
        lows[a, n] = (mid_scale[a][n : n + 1] * state[a]).astype(BF16)
        low_ref[heads[a], n] = lows[a, n]
        if n < blocks - 1:
            state[a] = end_scale[a][n : n + 1] * state[a] + rest_scale[a][n : n + 1] * updates[a, n]

    def combine(a, n):
        v = v_ref[span(n), lanes[a]]
        if n == 0:
            totals[a, n] = nn(weights[a, n], v)
        else:
            left = jnp.concatenate([weights[a, n], q_up[a, n]], axis=1)
            totals[a, n] = nn(left, jnp.concatenate([v, lows[a, n]], axis=0))

    def store(a, n):
        local_ref[span(n), lanes[a]] = totals[a, n].astype(BF16)

    staggered([scale, turn, multiply, mask_out, combine, store], steps)


def attend_body(first, count, load, *refs):
    k_ref, v_ref, cum_ref = refs[1:4]
    refs = refs[4:]
    copies = []
    if load == "queries":
        q_hbm, outs, (q_ref, sems) = refs[0], refs[1:8], refs[8:]
        for g in range(q_hbm.shape[1] // (GROUP * DH)):
            lanes = slice(g * GROUP * DH, (g + 1) * GROUP * DH)
            copies.append(pltpu.make_async_copy(q_hbm.at[:, lanes], q_ref.at[:, lanes], sems.at[g]))
    elif load == "grad_out":
        q_ref, go_hbm, outs, (go_ref, sems) = refs[0], refs[1], refs[9:16], refs[16:]
        copies.append(pltpu.make_async_copy(go_hbm, go_ref, sems.at[0]))
    else:
        q_ref, outs = refs[0], refs[8:15]
    for copy in copies:
        copy.start()
    both_masks = masks()
    picks = block_picks(k_ref.shape[0] // SPAN)
    held = []
    for at, copy in enumerate(copies):
        if load == "queries" and at * GROUP < first + count:
            copy.wait()
        else:
            held.append(copy)

    @pl.loop(0, count // PAIR)
    def _(at):
        heads = [first + at * PAIR + a for a in range(PAIR)]
        attend_heads(heads, q_ref, k_ref, v_ref, cum_ref, outs, both_masks, picks)

    for copy in held:
        copy.wait()


def attend(after, first, count, load, keys, values, cum, queries, grad_out, done):
    rows, width = keys.shape
    heads, blocks = width // DH, rows // SPAN
    like = jax.ShapeDtypeStruct((rows, width), BF16)
    squares = jax.ShapeDtypeStruct((heads, blocks, DH, DH), BF16)
    outs = [like, squares, jax.ShapeDtypeStruct((heads, DH, rows), BF16), like, like, like, squares]
    arrays, specs = [after, keys, values, cum, queries], [ANY, VMEM, VMEM, VMEM]
    specs.append(HBM if load == "queries" else VMEM)
    if load == "grad_out":
        arrays.append(grad_out)
        specs.append(HBM)
    aliases = {len(arrays) + i: i for i in range(len(done))}
    if load is not None:
        outs.append(like)
    return pl.pallas_call(
        functools.partial(attend_body, first, count, load),
        in_specs=specs + [VMEM] * len(done),
        out_specs=[VMEM] * len(outs),
        out_shape=outs,
        input_output_aliases=aliases,
        scratch_shapes=[] if load is None else [pltpu.SemaphoreType.DMA((heads // GROUP,))],
        compiler_params=params(6),
        cost_estimate=cost(10 * rows * count * DH * DH, 12 * rows * count * DH),
        name=f"attend_{first}",
    )(*arrays, *done)


def enter_body(of_other, q_ref, local_ref, go_ref, gain_ref, state_ref, cum_ref, before_ref, *refs):
    if of_other:
        attn_ref, low_ref, stats_ref, square_ref, inner_ref = refs[4:]
    else:
        attn_ref, low_ref, square_ref, inner_ref = refs
    core, _, _ = position()
    rows, width = q_ref.shape
    heads, blocks = width // DH, rows // SPAN
    if not of_other:
        square_ref[...] = jnp.zeros_like(square_ref)
        inner_ref[...] = jnp.zeros_like(inner_ref)

    for g in range(heads // 2 // GROUP):
        first = half_heads(core, of_other, g * GROUP, heads)
        lanes = [head_lanes(first + at) for at in range(GROUP)]
        carried, scales, gains = [], [], []
        for at in range(GROUP):
            low = piece_state(state_ref, g * GROUP + at).astype(BF16)
            low_ref[first + at] = low
            carried.append(nn(q_ref[:, lanes[at]], low))
            scales.append(jnp.exp(middle_lane(head_rows(cum_ref, first + at)) + head_rows(before_ref, first + at)))
            gains.append(gain_ref[:, lanes[at]])
        for n in range(blocks):
            square = square_ref[span(n), :]
            inner = inner_ref[span(n), :]
            for at in range(GROUP):
                entered = carried[at][span(n)] * scales[at][n : n + 1]
                attn = (local_ref[span(n), lanes[at]].astype(F32) + entered).astype(BF16)
                attn_ref[span(n), lanes[at]] = attn
                attn = attn.astype(F32)
                square += attn * attn
                inner += go_ref[span(n), lanes[at]].astype(F32) * gains[at] * attn
            square_ref[span(n), :] = square
            inner_ref[span(n), :] = inner

    if of_other:
        ones = jnp.ones((8, DH), F32)
        stats_ref[0:1, :] = dot(ones, square_ref[...], (1, 1), EXACT)[0:1]
        stats_ref[1:2, :] = dot(ones, inner_ref[...], (1, 1), EXACT)[0:1]


def attend_entering(of_other, queries, local, grad_out, gain, state, cum, before, done):
    rows, width = queries.shape
    heads = width // DH
    sums = jax.ShapeDtypeStruct((rows, DH), F32)
    outs = [jax.ShapeDtypeStruct((rows, width), BF16), jax.ShapeDtypeStruct((heads, DH, DH), BF16)]
    if of_other:
        outs, aliases = outs + [jax.ShapeDtypeStruct((2, rows), F32), sums, sums], {7: 0, 8: 1, 9: 3, 10: 4}
    else:
        outs, aliases = outs + [sums, sums], {}
    return pl.pallas_call(
        functools.partial(enter_body, of_other),
        in_specs=[VMEM] * (7 + len(done)),
        out_specs=[VMEM] * len(outs),
        out_shape=outs,
        input_output_aliases=aliases,
        compiler_params=params(4),
        cost_estimate=cost(rows * width * DH, 4 * rows * width),
        name="enter_taken" if of_other else "enter_kept",
    )(queries, local, grad_out, gain, state, cum, before, *done)


def columns(row, ref, blocks):
    for n in range(blocks):
        ref[span(n), :] = jnp.broadcast_to(row[:, span(n)], (SPAN, SPAN)).T


def norm_body(of_other, turned_ref, attn_ref, go_ref, gain_ref, cum_ref, before_ref, total_ref, *refs):
    core, _, _ = position()
    rows, width = attn_ref.shape
    heads, blocks = width // DH, rows // SPAN
    if of_other:
        stats_refs, (ga_ref, out_ref, inverse_ref, factor_ref) = refs[:-4], refs[-4:]
        stats = functools.reduce(jnp.add, [ref[...] for ref in stats_refs]) / (HEAD_TOTAL * DH)
        inverse = lax.rsqrt(stats[0:1] + 1e-06)
        columns(inverse, inverse_ref, blocks)
        columns(inverse * inverse * inverse * stats[1:2], factor_ref, blocks)
    else:
        inverse_ref, factor_ref, _, ga_ref, out_ref = refs

    for g in range(heads // 2 // GROUP):
        places = [g * GROUP + at for at in range(GROUP)]
        heads_now = [half_heads(core, of_other, place, heads) for place in places]
        lanes = [head_lanes(head) for head in heads_now]
        gains = [gain_ref[:, lane] for lane in lanes]
        gain_sums = [jnp.zeros((8, DH), F32) for _ in places]
        grads = [[] for _ in places]
        for n in range(blocks):
            for at in range(GROUP):
                attn = attn_ref[span(n), lanes[at]].astype(F32)
                scaled = go_ref[span(n), lanes[at]].astype(F32) * inverse_ref[span(n), :]
                gain_sums[at] += jnp.sum((scaled * attn).reshape(SPAN // 8, 8, DH), axis=0)
                grad = (scaled * gains[at] - attn * factor_ref[span(n), :]).astype(BF16)
                ga_ref[span(n), lanes[at]] = grad
                grads[at].append(grad)
        updates = [
            [nn(turned_ref[heads_now[at], :, span(n)], grads[at][n]) for n in range(blocks)] for at in range(GROUP)
        ]
        scales = [jnp.exp(middle_lane(head_rows(cum_ref, h)) + head_rows(before_ref, h)) for h in heads_now]
        states = [sum(scales[at][n : n + 1] * updates[at][n] for n in range(blocks)) for at in range(GROUP)]
        for at in range(GROUP):
            decay = jnp.exp(head_rows(total_ref, heads_now[at]))
            piece_store(out_ref, places[at], states[at], extra_rows(decay, jnp.sum(gain_sums[at], axis=0, keepdims=True)))


def norm_backward(of_other, turned, attn, grad_out, gain, cum, before, total, more):
    rows, width = attn.shape
    heads = width // DH
    pieces = jax.ShapeDtypeStruct((heads // 4, PIECE, DH), F32)
    cols = jax.ShapeDtypeStruct((rows, DH), F32)
    outs = [jax.ShapeDtypeStruct((rows, width), BF16), pieces] + ([cols, cols] if of_other else [])
    return pl.pallas_call(
        functools.partial(norm_body, of_other),
        in_specs=[VMEM] * (7 + len(more)),
        out_specs=[VMEM] * len(outs),
        out_shape=outs,
        input_output_aliases={} if of_other else {9: 0},
        compiler_params=params(5),
        cost_estimate=cost(rows * width * DH, 4 * rows * width),
        name="norm_given" if of_other else "norm_kept",
    )(turned, attn, grad_out, gain, cum, before, total, *more)


def grads_heads(heads, places, refs, out_ref, gq_ref, lk_ref, lv_ref, both_masks, picks):
    q_ref, k_ref, turned_ref, ks_ref, vs_ref, weights_ref, ga_ref, attn_ref = refs[:8]
    gain_ref, inverse_ref, low_ref, enter_ref, cum_ref, before_ref = refs[8:]
    mask, _ = both_masks
    blocks = k_ref.shape[0] // SPAN
    each = range(len(heads))
    steps = [(a, n) for n in range(blocks) for a in each]
    lanes = [head_lanes(h) for h in heads]
    here = [head_lanes(p) for p in places]
    cums = [head_rows(cum_ref, h) for h in heads]
    mids = [middle_lane(c) for c in cums]
    ends = [last_lane(c) for c in cums]
    query_scale = [jnp.exp(spread(c - m, picks)) for c, m in zip(cums, mids)]
    mid_scale, end_scale = [jnp.exp(m) for m in mids], [jnp.exp(e) for e in ends]
    rest_scale = [jnp.exp(e - m) for e, m in zip(ends, mids)]
    enter_scale = [jnp.exp(m + head_rows(before_ref, h)) for m, h in zip(mids, heads)]
    entering = [enter_ref[h].astype(F32) for h in heads]

    def at(ref, a, n):
        return ref[span(n), lanes[a]]

    ga_up, v_turned, states, scores, updates, weights, lows, lows_turned, grad_q, grad_k, grad_v = ({} for _ in range(11))
    back = {a: jnp.zeros((DH, DH), F32) for a in each}

    def scale(a, n):
        ga_up[a, n] = (at(ga_ref, a, n).astype(F32) * query_scale[a][:, span(n)]).astype(BF16)
        v_turned[a, n] = at(vs_ref, a, n).T
        state = low_ref[heads[a], n].astype(F32) + enter_scale[a][n : n + 1] * entering[a]
        states[a, n] = state.astype(BF16).T

    def multiply(a, n):
        scores[a, n] = nn(ga_up[a, n], v_turned[a, n])
        if n > 0:
            updates[a, n] = nn(turned_ref[heads[a], :, span(n)], at(ga_ref, a, n))

    def mask_out(a, n):
        scores[a, n] = jnp.where(mask, scores[a, n], 0.0).astype(BF16)
        weights[a, n] = scores[a, n].T
        if n < blocks - 1:
            lows[a, n] = (rest_scale[a][n : n + 1] * back[a]).astype(BF16)
            lows_turned[a, n] = lows[a, n].T
        if n > 0:
            back[a] = end_scale[a][n : n + 1] * back[a] + mid_scale[a][n : n + 1] * updates[a, n]

    def combine(a, n):
        left = jnp.concatenate([scores[a, n], ga_up[a, n]], axis=1)
        grad_q[a, n] = nn(left, jnp.concatenate([at(k_ref, a, n), states[a, n]], axis=0))
        left_k, right_k = weights[a, n], at(q_ref, a, n)
        left_v, right_v = weights_ref[heads[a], n], at(ga_ref, a, n)
        if n < blocks - 1:
            left_k = jnp.concatenate([left_k, at(vs_ref, a, n)], axis=1)
            right_k = jnp.concatenate([right_k, lows_turned[a, n]], axis=0)
            left_v = jnp.concatenate([left_v, at(ks_ref, a, n)], axis=1)
            right_v = jnp.concatenate([right_v, lows[a, n]], axis=0)
        grad_k[a, n] = nn(left_k, right_k)
        grad_v[a, n] = nn(left_v, right_v)

    def store(a, n):
        gq_ref[span(n), here[a]] = grad_q[a, n].astype(BF16)
        lv_ref[span(n), lanes[a]] = grad_v[a, n].astype(BF16)
        lk_ref[span(n), lanes[a]] = grad_k[a, n].astype(BF16)
        normed = at(attn_ref, a, n).astype(F32) * inverse_ref[span(n), :]
        out_ref[span(n), here[a]] = (normed * gain_ref[:, lanes[a]]).astype(BF16)

    staggered([scale, multiply, mask_out, combine, store], steps[::-1])


def grads_body(first, count, chained, *refs):
    inputs = refs[1:15]
    refs = refs[15 + (4 if chained else 0) :]
    out_hbm, gq_hbm, lk_ref, lv_ref, out_ref, gq_ref, sems = refs
    both_masks = masks()
    picks = block_picks(inputs[0].shape[0] // SPAN)

    def copies(at):
        here, there = head_lanes(at * PAIR, PAIR), head_lanes(first + at * PAIR, PAIR)
        return [
            pltpu.make_async_copy(out_ref.at[:, here], out_hbm.at[:, there], sems.at[0, at]),
            pltpu.make_async_copy(gq_ref.at[:, here], gq_hbm.at[:, there], sems.at[1, at]),
        ]

    @pl.loop(0, count // PAIR)
    def _(at):
        places = [at * PAIR + a for a in range(PAIR)]
        heads = [first + p for p in places]
        grads_heads(heads, places, inputs, out_ref, gq_ref, lk_ref, lv_ref, both_masks, picks)
        for copy in copies(at):
            copy.start()

    @pl.loop(0, count // PAIR)
    def _(at):
        for copy in copies(at):
            copy.wait()


def grads_local(after, first, count, inputs, done):
    rows, width = inputs[0].shape
    like = jax.ShapeDtypeStruct((rows, width), BF16)
    kinds = [HBM, HBM, VMEM, VMEM]
    return pl.pallas_call(
        functools.partial(grads_body, first, count, bool(done)),
        in_specs=[ANY] + [VMEM] * 14 + (kinds if done else []),
        out_specs=kinds,
        out_shape=[like] * 4,
        input_output_aliases={15 + i: i for i in range(4)} if done else {},
        scratch_shapes=[
            pltpu.VMEM((rows, count * DH), BF16),
            pltpu.VMEM((rows, count * DH), BF16),
            pltpu.SemaphoreType.DMA((2, count // PAIR)),
        ],
        compiler_params=params(8),
        cost_estimate=cost(22 * rows * count * DH * DH, 24 * rows * count * DH),
        name=f"grads_{first}",
    )(after, *inputs, *done)


def leave_body(of_other, k_ref, v_ref, lk_ref, lv_ref, state_ref, cum_ref, before_ref, total_ref, *refs):
    core, _, _ = position()
    rows, width = k_ref.shape
    heads, blocks = width // DH, rows // SPAN
    half = heads // 2
    copies = []
    if of_other:
        kept_k_ref, kept_v_ref, kept_gain_ref, gk_hbm, gv_hbm, gg_ref, gk_ref, gv_ref, sems, kept_sems = refs
        there = head_lanes(half_heads(core, False, 0, heads), half)
        for which, (source, target) in enumerate(((kept_k_ref, gk_hbm), (kept_v_ref, gv_hbm))):
            copies.append(pltpu.make_async_copy(source, target.at[:, there], kept_sems.at[which]))
            copies[-1].start()
        gg_ref[...] = kept_gain_ref[...]
    else:
        gk_ref, gv_ref, gg_ref = refs
    for g in range(half // GROUP):

        for at in range(g * GROUP // PAIR, (g + 1) * GROUP // PAIR):
            first = half_heads(core, of_other, at * PAIR, heads)
            lanes = [head_lanes(first + a) for a in range(PAIR)]
            here = [head_lanes(at * PAIR + a) for a in range(PAIR)]
            lows = [piece_state(state_ref, at * PAIR + a).astype(BF16) for a in range(PAIR)]
            from_v = [nt(v_ref[:, lanes[a]], lows[a]) for a in range(PAIR)]
            from_k = [nn(k_ref[:, lanes[a]], lows[a]) for a in range(PAIR)]
            scales = [
                jnp.exp(
                    head_rows(total_ref, first + a)
                    - head_rows(before_ref, first + a)
                    - middle_lane(head_rows(cum_ref, first + a))
                )
                for a in range(PAIR)
            ]
            for n in range(blocks):
                for a in range(PAIR):
                    factor = scales[a][n : n + 1]
                    grad_k = lk_ref[span(n), lanes[a]].astype(F32) + factor * from_v[a][span(n)]
                    grad_v = lv_ref[span(n), lanes[a]].astype(F32) + factor * from_k[a][span(n)]
                    gk_ref[span(n), here[a]] = grad_k.astype(BF16)
                    gv_ref[span(n), here[a]] = grad_v.astype(BF16)
            for a in range(PAIR):
                row = STATES + 4 * (a % 2) + 1
                gg_ref[:, lanes[a]] = state_ref[at * PAIR // 2 + a // 2, row : row + 1, :]

        if of_other:
            here = slice(g * GROUP * DH, (g + 1) * GROUP * DH)
            there = head_lanes(half_heads(core, True, g * GROUP, heads), GROUP)
            for which, (source, target) in enumerate(((gk_ref, gk_hbm), (gv_ref, gv_hbm))):
                copies.append(pltpu.make_async_copy(source.at[:, here], target.at[:, there], sems.at[which, g]))
                copies[-1].start()
    for copy in copies:
        copy.wait()


def grads_leaving(of_other, keys, values, local_k, local_v, state, cum, before, total, done):
    rows, width = keys.shape
    heads = width // DH
    like = jax.ShapeDtypeStruct((rows, width if of_other else width // 2), BF16)
    kept = pltpu.VMEM((rows, width // 2), BF16)
    sems = [pltpu.SemaphoreType.DMA((2, heads // 2 // GROUP)), pltpu.SemaphoreType.DMA((2,))]
    return pl.pallas_call(
        functools.partial(leave_body, of_other),
        in_specs=[VMEM] * (8 + len(done)),
        out_specs=[HBM, HBM, VMEM] if of_other else [VMEM] * 3,
        out_shape=[like, like, jax.ShapeDtypeStruct((1, width), F32)],
        scratch_shapes=[kept, kept] + sems if of_other else [],
        compiler_params=params(6),
        cost_estimate=cost(2 * rows * width * DH, 6 * rows * width),
        name="leave_taken" if of_other else "leave_kept",
    )(keys, values, local_k, local_v, state, cum, before, total, *done)


def per_device(queries, keys, values, log_decay, gain, grad_out):
    gain_row = gain.reshape(1, -1)
    keys, values, queries, grad_out, log_decay = (
        pltpu.with_memory_space_constraint(a, pltpu.HBM) for a in (keys, values, queries, grad_out, log_decay)
    )
    send, keys, values, cum, before, total = local_state(True, keys, values, (log_decay,))
    (own,) = local_state(False, keys, values, (cum, before, total))

    def attend_part(first, count, load):
        def run(after, done):
            held = done[7] if done else queries
            outs = attend(after, first, count, load, keys, values, cum, held, grad_out, done[:7])
            if load == "queries":
                return (*outs[:7], outs[7], outs[0])
            if load == "grad_out":
                return (*outs[:7], held, outs[7], outs[0])
            return (*outs[:7], held, done[8], outs[0])

        return run

    keep, taken, (local, lows, turned, q_up, k_up, v_up, weights, queries, grad_out, _) = scan_over_seq(
        send, own, False, [attend_part(0, 6, "queries"), attend_part(6, 6, "grad_out"), attend_part(12, 4, None)]
    )
    table = (cum, before)
    done = attend_entering(False, q_up, local, grad_out, gain_row, keep, *table, ())
    attn, entering, stats = attend_entering(True, q_up, local, grad_out, gain_row, taken, *table, done)[:3]
    count = lax.axis_size("head")
    stats = [stats] + [
        lax.ppermute(stats, "head", [(i, (i + s) % count) for i in range(count)]) for s in arrival_order(count)[1:]
    ]
    shared = (turned, attn, grad_out, gain_row, cum, before, total)
    grad_attn, send, inverse, factor = norm_backward(True, *shared, stats)
    grad_attn, own = norm_backward(False, *shared, (inverse, factor, grad_attn))
    inputs = (queries, keys, turned, k_up, v_up, weights, grad_attn, attn, gain_row, inverse, lows, entering, cum, before)

    def grads_part(first, count):
        return lambda after, done: grads_local(after, first, count, inputs, done)

    keep, taken, (output, grad_q, local_k, local_v) = scan_over_seq(
        send, own, True, [grads_part(0, 6), grads_part(6, 6), grads_part(12, 4)]
    )
    shared = (k_up, v_up, local_k, local_v)
    done = grads_leaving(False, *shared, keep, cum, before, total, ())
    grad_k, grad_v, grad_gain = grads_leaving(True, *shared, taken, cum, before, total, done)
    return output, grad_q, grad_k, grad_v, grad_gain.reshape(-1)


def solution(mesh):
    tokens, heads = P("seq", "head"), P("head")
    return jax.shard_map(
        per_device,
        mesh=mesh,
        in_specs=(tokens, tokens, tokens, P("head", "seq"), heads, tokens),
        out_specs=(tokens, tokens, tokens, tokens, heads),
        check_vma=False,
    )
```

profile of v0, /device:TPU:1, one launch (start us, length us, event | category | flops | bytes accessed | tf_op | source)
XLA Modules:
  0.0 93.8 jit_solution(8124060354565050576)
XLA Ops:
  0.6 2.9 %state_given.1 = (f32[4,264,128]{2,1,0:T(8,128)S(1)}, bf16[768,2048]{1,0:T(8,128)(2,1)S(1)}, bf16[768,2048]{1,0:T(8,128)(2,1)S(1)}, f32[128,128]{1,0:T(8,128)S(1...) custom-call(bf16[768,2048]{1,0:T(8,128)(2,1)} %refs_0_.1, bf16[768,2048]{1,0:T(8,128)(2,1)} %refs_1_.1, f32[16,768]{1,0:T(8,128)} %refs_2_.1), custom_call_target="tpu_custom_call" | custom-call | flops 201326592 | bytes 3145728 | tf_op jit(solution)/shard_map/state_given/pallas_call | solution.py:183
  3.6 1.5 %collective-permute-start = (f32[4,264,128]{2,1,0:T(8,128)S(1)}, f32[4,264,128]{2,1,0:T(8,128)S(1)}, u32[]{:S(2)}, u32[]{:S(2)}) collective-permute-start(f32[4,264,128]{2,1,0:T(8,128)S(1)} %get-tuple-element.94), channel_id=1, source_target_pairs={{0,4},{4,0},{8,12},{12,8},{16,20},{20,16},{24,28},{28,24},{32,36},... | collective-permute-start | bytes 1622024 | tf_op jit(solution)/shard_map/ppermute | solution.py:303
  5.1 1.2 %state_kept.1.own_ref.refs_4_ = f32[4,264,128]{2,1,0:T(8,128)S(1)} custom-call(bf16[768,2048]{1,0:T(8,128)(2,1)S(1)} %get-tuple-element.89.refs_0_.refs_1_.refs_2_, bf16[768,2048]{1,0:T(8,128)(2,1)S(1)} %get-tuple-element.90.refs_1_.refs_2_, f32[128,128]{1,0:T(8,128)S(1)} %get-tuple-element.91.refs_2_.refs_3_.cum_ref.refs_13_, ...), custom_call_target="tpu_custom_call" | custom-call | flops 201326592 | bytes 3145728 | tf_op jit(solution)/shard_map/state_kept/pallas_call | solution.py:183
  6.3 0.4 collective-permute-done.got_ref.refs_5_
  6.7 3.8 %collective-permute-start.1 = (f32[264,128]{1,0:T(8,128)S(1)}, f32[264,128]{1,0:T(8,128)S(1)}, u32[]{:S(2)}, u32[]{:S(2)}) collective-permute-start(f32[264,128]{1,0:T(8,128)S(1)} %get-tuple-element.96), channel_id=1, source_target_pairs={{0,16},{4,20},{8,24},{12,28},{16,0},{20,4},{24,8},{28,12},{32,48},... | collective-permute-start | bytes 405512 | tf_op jit(solution)/shard_map/ppermute | solution.py:301
  10.5 0.7 collective-permute-start.2
  11.2 1.9 %collective-permute-start.3 = (f32[264,128]{1,0:T(8,128)S(1)}, f32[264,128]{1,0:T(8,128)S(1)}, u32[]{:S(2)}, u32[]{:S(2)}) collective-permute-start(f32[264,128]{1,0:T(8,128)S(1)} %get-tuple-element.98), channel_id=1, source_target_pairs={{0,24},{4,28},{8,0},{12,4},{16,8},{20,12},{24,16},{28,20},{32,56},... | collective-permute-start | bytes 405512 | tf_op jit(solution)/shard_map/ppermute | solution.py:301
  13.2 6.0 %attend_0.1 = (bf16[768,2048]{1,0:T(8,128)(2,1)S(1)}, bf16[16,6,128,128]{3,2,1,0:T(8,128)(2,1)S(1)}, bf16[16,128,768]{2,1,0:T(8,128)(2,1)S(1)}, bf16[768,2048]{1...) custom-call(f32[264,128]{1,0:T(8,128)S(1)} %get-tuple-element.95.ref, ...), custom_call_target="tpu_custom_call" | custom-call | flops 754974720 | bytes 7077888 | tf_op jit(solution)/shard_map/attend_0/pallas_call | solution.py:451
  19.3 2.8 %collective-permute-start.4 = (f32[264,128]{1,0:T(8,128)S(1)}, f32[264,128]{1,0:T(8,128)S(1)}, u32[]{:S(2)}, u32[]{:S(2)}) collective-permute-start(f32[264,128]{1,0:T(8,128)S(1)} %get-tuple-element.100.refs_0_), channel_id=1, source_target_pairs={{0,64},{4,68},{8,72},{12,76},{16,80},{20,84},{24,88},{28,92},{32,9... | collective-permute-start | bytes 405512 | tf_op jit(solution)/shard_map/ppermute | solution.py:301
  22.1 0.3 collective-permute-start.5
  22.5 2.4 %collective-permute-start.6 = (f32[264,128]{1,0:T(8,128)S(1)}, f32[264,128]{1,0:T(8,128)S(1)}, u32[]{:S(2)}, u32[]{:S(2)}) collective-permute-start(f32[264,128]{1,0:T(8,128)S(1)} %get-tuple-element.100.refs_0_), channel_id=1, source_target_pairs={{0,96},{4,100},{8,104},{12,108},{16,112},{20,116},{24,120},{28,124... | collective-permute-start | bytes 405512 | tf_op jit(solution)/shard_map/ppermute | solution.py:301
  24.8 4.6 %attend_6.1 = (bf16[768,2048]{1,0:T(8,128)(2,1)S(1)}, bf16[16,6,128,128]{3,2,1,0:T(8,128)(2,1)S(1)}, bf16[16,128,768]{2,1,0:T(8,128)(2,1)S(1)}, bf16[768,2048]{1...) custom-call(f32[264,128]{1,0:T(8,128)S(1)} %get-tuple-element.100.re, ...), custom_call_target="tpu_custom_call", output_to_operand_aliasing={{0}: (6, {}), {1}: (7, {}), {2}: (8, {}), {3}: (9, {}), {4}... | custom-call | flops 754974720 | bytes 7077888 | tf_op jit(solution)/shard_map/attend_6/pallas_call | solution.py:451
  29.5 0.2 join_x.2
  29.7 0.4 collective-permute-start.7
  30.1 1.0 %collective-permute-start.8 = (f32[256,128]{1,0:T(8,128)S(1)}, f32[256,128]{1,0:T(8,128)S(1)}, u32[]{:S(2)}, u32[]{:S(2)}) collective-permute-start(f32[256,128]{1,0:T(8,128)S(1)} %get-tuple-element.122), channel_id=1, source_target_pairs={{0,8},{4,12},{8,16},{12,20},{16,24},{20,28},{24,0},{28,4},{32,40},... | collective-permute-start | bytes 393224 | tf_op jit(solution)/shard_map/ppermute | solution.py:301
  31.1 1.7 %collective-permute-start.9 = (f32[256,128]{1,0:T(8,128)S(1)}, f32[256,128]{1,0:T(8,128)S(1)}, u32[]{:S(2)}, u32[]{:S(2)}) collective-permute-start(f32[256,128]{1,0:T(8,128)S(1)} %get-tuple-element.123), channel_id=1, source_target_pairs={{0,24},{4,28},{8,0},{12,4},{16,8},{20,12},{24,16},{28,20},{32,56},... | collective-permute-start | bytes 393224 | tf_op jit(solution)/shard_map/ppermute | solution.py:301
  32.7 3.1 %attend_12.1 = (bf16[768,2048]{1,0:T(8,128)(2,1)S(1)}, bf16[16,6,128,128]{3,2,1,0:T(8,128)(2,1)S(1)}, bf16[16,128,768]{2,1,0:T(8,128)(2,1)S(1)}, bf16[768,2048]{...) custom-call(f32[256,128]{1,0:T(8,128)S(1)} %get-tuple-element.110.re, ...), custom_call_target="tpu_custom_call", output_to_operand_aliasing={{0}: (5, {}), {1}: (6, {}), {2}: (7, {}), {3}: (8, {}), {4}... | custom-call | flops 503316480 | bytes 4718592 | tf_op jit(solution)/shard_map/attend_12/pallas_call | solution.py:451
  35.9 2.5 %collective-permute-done.8.refs_2_ = f32[256,128]{1,0:T(8,128)S(1)} collective-permute-done((f32[256,128]{1,0:T(8,128)S(1)}, f32[256,128]{1,0:T(8,128)S(1)}, u32[]{:S(2)}, u32[]{:S(2)}) %collective-permute-start.8) | collective-permute-done | bytes 131104 | tf_op jit(solution)/shard_map/ppermute | solution.py:301
  38.5 1.9 %collective-permute-start.10 = (f32[4,256,128]{2,1,0:T(8,128)S(1)}, f32[4,256,128]{2,1,0:T(8,128)S(1)}, u32[]{:S(2)}, u32[]{:S(2)}) collective-permute-start(f32[4,256,128]{2,1,0:T(8,128)S(1)} %get-tuple-element.124), channel_id=1, source_target_pairs={{0,4},{4,0},{8,12},{12,8},{16,20},{20,16},{24,28},{28,24},{32,36},... | collective-permute-start | bytes 1572872 | tf_op jit(solution)/shard_map/ppermute | solution.py:322
  40.4 1.7 %enter_kept.1 = (bf16[768,2048]{1,0:T(8,128)(2,1)S(1)}, bf16[16,128,128]{2,1,0:T(8,128)(2,1)S(1)}, f32[768,128]{1,0:T(8,128)S(1)}, f32[768,128]{1,0:T(8,128)S(1)}) custom-call(bf16[768,2048]{1,0:T(8,128)(2,1)S(1)} %get-tuple-element.118.q_ref, bf16[768,2048]{1,0:T(8,128)(2,1)S(1)} %get-tuple-element.119.refs_6_.local_ref, ...), custom_call_target="tpu_custom_call" | custom-call | flops 201326592 | bytes 6291456 | tf_op jit(solution)/shard_map/enter_kept/pallas_call | solution.py:514
  42.1 2.4 %enter_taken.1 = (bf16[768,2048]{1,0:T(8,128)(2,1)S(1)}, bf16[16,128,128]{2,1,0:T(8,128)(2,1)S(1)}, f32[2,768]{1,0:T(2,128)S(1)}, f32[768,128]{1,0:T(8,128)S(1)}, f32[768,128]{1,0:T(8,128)S(1)}) custom-call(bf16[768,2048]{1,0:T(8,128)(2,1)S(1)} %get-tuple-element.118.q_ref, ...), custom_call_target="tpu_custom_call", output_to_operand_aliasing={{0}: (7, {}), {1}: (8, {}), {3}: (9, {}), {4}: (10, {})} | custom-call | flops 201326592 | bytes 6291456 | tf_op jit(solution)/shard_map/enter_taken/pallas_call | solution.py:514
  44.5 2.9 %collective-permute-start.11 = (f32[2,768]{1,0:T(2,128)S(1)}, f32[2,768]{1,0:T(2,128)S(1)}, u32[]{:S(2)}, u32[]{:S(2)}) collective-permute-start(f32[2,768]{1,0:T(2,128)S(1)} %get-tuple-element.131.refs_0_), channel_id=1, source_target_pairs={{0,2},{1,3},{2,0},{3,1},{4,6},{5,7},{6,4},{7,5},{8,10},{9,11},{10,... | collective-permute-start | bytes 18440 | tf_op jit(solution)/shard_map/ppermute | solution.py:802
  47.5 0.4 collective-permute-start.12
  47.9 2.3 %collective-permute-start.13 = (f32[2,768]{1,0:T(2,128)S(1)}, f32[2,768]{1,0:T(2,128)S(1)}, u32[]{:S(2)}, u32[]{:S(2)}) collective-permute-start(f32[2,768]{1,0:T(2,128)S(1)} %get-tuple-element.131.refs_0_), channel_id=1, source_target_pairs={{0,3},{1,0},{2,1},{3,2},{4,7},{5,4},{6,5},{7,6},{8,11},{9,8},{10,9... | collective-permute-start | bytes 18440 | tf_op jit(solution)/shard_map/ppermute | solution.py:802
  50.1 1.0 %collective-permute-done.12.refs_2_ = f32[2,768]{1,0:T(2,128)S(1)} collective-permute-done((f32[2,768]{1,0:T(2,128)S(1)}, f32[2,768]{1,0:T(2,128)S(1)}, u32[]{:S(2)}, u32[]{:S(2)}) %collective-permute-start.12) | collective-permute-done | bytes 6176 | tf_op jit(solution)/shard_map/ppermute | solution.py:802
  51.1 1.9 %norm_given.1 = (bf16[768,2048]{1,0:T(8,128)(2,1)S(1)}, f32[4,264,128]{2,1,0:T(8,128)S(1)}, f32[768,128]{1,0:T(8,128)S(1)}, f32[768,128]{1,0:T(8,128)S(1)}) custom-call(bf16[16,128,768]{2,1,0:T(8,128)(2,1)S(1)} %get-tuple-element.117.turned_ref.refs_3_, bf16[768,2048]{1,0:T(8,128)(2,1)S(1)} %get-tuple-element.130.attn_ref.refs_8_, ...), custom_call_target="tpu_custom_call" | custom-call | flops 201326592 | bytes 6291456 | tf_op jit(solution)/shard_map/norm_given/pallas_call | solution.py:575
  53.0 1.7 %collective-permute-start.14 = (f32[4,264,128]{2,1,0:T(8,128)S(1)}, f32[4,264,128]{2,1,0:T(8,128)S(1)}, u32[]{:S(2)}, u32[]{:S(2)}) collective-permute-start(f32[4,264,128]{2,1,0:T(8,128)S(1)} %get-tuple-element.136), channel_id=1, source_target_pairs={{0,4},{4,0},{8,12},{12,8},{16,20},{20,16},{24,28},{28,24},{32,36},... | collective-permute-start | bytes 1622024 | tf_op jit(solution)/shard_map/ppermute | solution.py:303
  54.7 1.8 %norm_kept.1 = (bf16[768,2048]{1,0:T(8,128)(2,1)S(1)}, f32[4,264,128]{2,1,0:T(8,128)S(1)}) custom-call(bf16[16,128,768]{2,1,0:T(8,128)(2,1)S(1)} %get-tuple-element.117.turned_ref.refs_3_, bf16[768,2048]{1,0:T(8,128)(2,1)S(1)} %get-tuple-element.130.attn_ref.refs_8_, ...), custom_call_target="tpu_custom_call", output_to_operand_aliasing={{0}: (9, {})} | custom-call | flops 201326592 | bytes 6291456 | tf_op jit(solution)/shard_map/norm_kept/pallas_call | solution.py:575
  56.6 0.5 collective-permute-start.15
  57.2 1.4 %collective-permute-start.16 = (f32[264,128]{1,0:T(8,128)S(1)}, f32[264,128]{1,0:T(8,128)S(1)}, u32[]{:S(2)}, u32[]{:S(2)}) collective-permute-start(f32[264,128]{1,0:T(8,128)S(1)} %get-tuple-element.139), channel_id=1, source_target_pairs={{0,8},{4,12},{8,16},{12,20},{16,24},{20,28},{24,0},{28,4},{32,40},... | collective-permute-start | bytes 405512 | tf_op jit(solution)/shard_map/ppermute | solution.py:301
  58.6 1.3 %collective-permute-start.17 = (f32[264,128]{1,0:T(8,128)S(1)}, f32[264,128]{1,0:T(8,128)S(1)}, u32[]{:S(2)}, u32[]{:S(2)}) collective-permute-start(f32[264,128]{1,0:T(8,128)S(1)} %get-tuple-element.140), channel_id=1, source_target_pairs={{0,24},{4,28},{8,0},{12,4},{16,8},{20,12},{24,16},{28,20},{32,56},... | collective-permute-start | bytes 405512 | tf_op jit(solution)/shard_map/ppermute | solution.py:301
  59.9 5.8 %grads_0.1 = (bf16[768,2048]{1,0:T(8,128)(2,1)}, bf16[768,2048]{1,0:T(8,128)(2,1)}, bf16[768,2048]{1,0:T(8,128)(2,1)S(1)}, bf16[768,2048]{1,0:T(8,128)(2,1)S(1)}) custom-call(f32[264,128]{1,0:T(8,128)S(1)} %get-tuple-element.137.refs_0_, bf16[768,2048]{1,0:T(8,128)(2,1)S(1)} %get-tuple-element.102.refs_4_.refs_1_, ...), custom_call_target="tpu_custom_call" | custom-call | flops 1660944384 | bytes 14155776 | tf_op jit(solution)/shard_map/grads_0/pallas_call | solution.py:686
  65.7 1.0 %collective-permute-done.16.refs_2_ = f32[264,128]{1,0:T(8,128)S(1)} collective-permute-done((f32[264,128]{1,0:T(8,128)S(1)}, f32[264,128]{1,0:T(8,128)S(1)}, u32[]{:S(2)}, u32[]{:S(2)}) %collective-permute-start.16) | collective-permute-done | bytes 135200 | tf_op jit(solution)/shard_map/ppermute | solution.py:301
  66.7 0.7 collective-permute-start.18
  67.4 1.7 %collective-permute-start.19 = (f32[264,128]{1,0:T(8,128)S(1)}, f32[264,128]{1,0:T(8,128)S(1)}, u32[]{:S(2)}, u32[]{:S(2)}) collective-permute-start(f32[264,128]{1,0:T(8,128)S(1)} %get-tuple-element.148.refs_0_), channel_id=1, source_target_pairs={{0,32},{4,36},{8,40},{12,44},{16,48},{20,52},{24,56},{28,60},{32,6... | collective-permute-start | bytes 405512 | tf_op jit(solution)/shard_map/ppermute | solution.py:301
  69.2 0.9 %collective-permute-start.20 = (f32[264,128]{1,0:T(8,128)S(1)}, f32[264,128]{1,0:T(8,128)S(1)}, u32[]{:S(2)}, u32[]{:S(2)}) collective-permute-start(f32[264,128]{1,0:T(8,128)S(1)} %get-tuple-element.148.refs_0_), channel_id=1, source_target_pairs={{0,96},{4,100},{8,104},{12,108},{16,112},{20,116},{24,120},{28,124... | collective-permute-start | bytes 405512 | tf_op jit(solution)/shard_map/ppermute | solution.py:301
  70.1 5.8 %grads_6.1 = (bf16[768,2048]{1,0:T(8,128)(2,1)}, bf16[768,2048]{1,0:T(8,128)(2,1)}, bf16[768,2048]{1,0:T(8,128)(2,1)S(1)}, bf16[768,2048]{1,0:T(8,128)(2,1)S(1)}) custom-call(f32[264,128]{1,0:T(8,128)S(1)} %get-tuple-element.148.refs_0_, ...), custom_call_target="tpu_custom_call", output_to_operand_aliasing={{0}: (15, {}), {1}: (16, {}), {2}: (17, {}), {3}: (18, {})} | custom-call | flops 1660944384 | bytes 14155776 | tf_op jit(solution)/shard_map/grads_6/pallas_call | solution.py:686
  75.9 0.8 collective-permute-done.19.refs_2_
  76.7 0.2 join_x.3
  76.9 0.4 collective-permute-start.21
  77.3 1.5 %collective-permute-start.22 = (f32[264,128]{1,0:T(8,128)S(1)}, f32[264,128]{1,0:T(8,128)S(1)}, u32[]{:S(2)}, u32[]{:S(2)}) collective-permute-start(f32[264,128]{1,0:T(8,128)S(1)} %get-tuple-element.163), channel_id=1, source_target_pairs={{0,8},{4,12},{8,16},{12,20},{16,24},{20,28},{24,0},{28,4},{32,40},... | collective-permute-start | bytes 405512 | tf_op jit(solution)/shard_map/ppermute | solution.py:301
  78.8 1.2 %collective-permute-start.23 = (f32[264,128]{1,0:T(8,128)S(1)}, f32[264,128]{1,0:T(8,128)S(1)}, u32[]{:S(2)}, u32[]{:S(2)}) collective-permute-start(f32[264,128]{1,0:T(8,128)S(1)} %get-tuple-element.164), channel_id=1, source_target_pairs={{0,24},{4,28},{8,0},{12,4},{16,8},{20,12},{24,16},{28,20},{32,56},... | collective-permute-start | bytes 405512 | tf_op jit(solution)/shard_map/ppermute | solution.py:301
  80.0 4.1 %grads_12.1 = (bf16[768,2048]{1,0:T(8,128)(2,1)}, bf16[768,2048]{1,0:T(8,128)(2,1)}, bf16[768,2048]{1,0:T(8,128)(2,1)S(1)}, bf16[768,2048]{1,0:T(8,128)(2,1)S(1)}) custom-call(f32[264,128]{1,0:T(8,128)S(1)} %get-tuple-element.154.refs_0_, ...), custom_call_target="tpu_custom_call", output_to_operand_aliasing={{0}: (15, {}), {1}: (16, {}), {2}: (17, {}), {3}: (18, {})} | custom-call | flops 1107296256 | bytes 9437184 | tf_op jit(solution)/shard_map/grads_12/pallas_call | solution.py:686
  84.2 2.7 %collective-permute-done.22.refs_2_ = f32[264,128]{1,0:T(8,128)S(1)} collective-permute-done((f32[264,128]{1,0:T(8,128)S(1)}, f32[264,128]{1,0:T(8,128)S(1)}, u32[]{:S(2)}, u32[]{:S(2)}) %collective-permute-start.22) | collective-permute-done | bytes 135200 | tf_op jit(solution)/shard_map/ppermute | solution.py:301
  86.9 0.1 entering.3
  87.0 0.6 collective-permute-start.24
  87.6 1.8 %leave_kept.1 = (bf16[768,1024]{1,0:T(8,128)(2,1)S(1)}, bf16[768,1024]{1,0:T(8,128)(2,1)S(1)}, f32[1,2048]{1,0:T(1,128)S(1)}) custom-call(bf16[768,2048]{1,0:T(8,128)(2,1)S(1)} %get-tuple-element.141.refs_4_.k_ref, bf16[768,2048]{1,0:T(8,128)(2,1)S(1)} %get-tuple-element.142.refs_5_.v_ref, bf16[768,2048]{1,0:T(8,128)(2,1)S(1)} %get-tuple-element.160.lk_ref, ...), custom_call_target="tpu_custom_call" | custom-call | flops 402653184 | bytes 9437184 | tf_op jit(solution)/shard_map/leave_kept/pallas_call | solution.py:762
  89.4 4.2 %leave_taken.1 = (bf16[768,2048]{1,0:T(8,128)(2,1)}, bf16[768,2048]{1,0:T(8,128)(2,1)}, f32[1,2048]{1,0:T(1,128)}) custom-call(bf16[768,2048]{1,0:T(8,128)(2,1)S(1)} %get-tuple-element.141.refs_4_.k_ref, bf16[768,2048]{1,0:T(8,128)(2,1)S(1)} %get-tuple-element.142.refs_5_.v_ref, bf16[768,2048]{1,0:T(8,128)(2,1)S(1)} %get-tuple-element.160.lk_ref, ...), custom_call_target="tpu_custom_call" | custom-call | flops 402653184 | bytes 9437184 | tf_op jit(solution)/shard_map/leave_taken/pallas_call | solution.py:762
  (26 shorter events, 0.6 us)
Async XLA Ops:
  3.6 3.1 %collective-permute-start = (f32[4,264,128]{2,1,0:T(8,128)S(1)}, f32[4,264,128]{2,1,0:T(8,128)S(1)}, u32[]{:S(2)}, u32[]{:S(2)}) collective-permute-start(f32[4,264,128]{2,1,0:T(8,128)S(1)} %get-tuple-element.94), channel_id=1, source_target_pairs={{0,4},{4,0},{8,12},{12,8},{16,20},{20,16},{24,28},{28,24},{32,36},... | collective-permute-start | bytes 1622024 | tf_op jit(solution)/shard_map/ppermute | solution.py:303
  6.7 12.4 %collective-permute-start.1 = (f32[264,128]{1,0:T(8,128)S(1)}, f32[264,128]{1,0:T(8,128)S(1)}, u32[]{:S(2)}, u32[]{:S(2)}) collective-permute-start(f32[264,128]{1,0:T(8,128)S(1)} %get-tuple-element.96), channel_id=1, source_target_pairs={{0,16},{4,20},{8,24},{12,28},{16,0},{20,4},{24,8},{28,12},{32,48},... | collective-permute-start | bytes 405512 | tf_op jit(solution)/shard_map/ppermute | solution.py:301
  10.5 8.7 %collective-permute-start.2 = (f32[264,128]{1,0:T(8,128)S(1)}, f32[264,128]{1,0:T(8,128)S(1)}, u32[]{:S(2)}, u32[]{:S(2)}) collective-permute-start(f32[264,128]{1,0:T(8,128)S(1)} %get-tuple-element.97), channel_id=1, source_target_pairs={{0,8},{4,12},{8,16},{12,20},{16,24},{20,28},{24,0},{28,4},{32,40},... | collective-permute-start | bytes 405512 | tf_op jit(solution)/shard_map/ppermute | solution.py:301
  11.2 8.0 %collective-permute-start.3 = (f32[264,128]{1,0:T(8,128)S(1)}, f32[264,128]{1,0:T(8,128)S(1)}, u32[]{:S(2)}, u32[]{:S(2)}) collective-permute-start(f32[264,128]{1,0:T(8,128)S(1)} %get-tuple-element.98), channel_id=1, source_target_pairs={{0,24},{4,28},{8,0},{12,4},{16,8},{20,12},{24,16},{28,20},{32,56},... | collective-permute-start | bytes 405512 | tf_op jit(solution)/shard_map/ppermute | solution.py:301
  19.3 10.2 %collective-permute-start.4 = (f32[264,128]{1,0:T(8,128)S(1)}, f32[264,128]{1,0:T(8,128)S(1)}, u32[]{:S(2)}, u32[]{:S(2)}) collective-permute-start(f32[264,128]{1,0:T(8,128)S(1)} %get-tuple-element.100.refs_0_), channel_id=1, source_target_pairs={{0,64},{4,68},{8,72},{12,76},{16,80},{20,84},{24,88},{28,92},{32,9... | collective-permute-start | bytes 405512 | tf_op jit(solution)/shard_map/ppermute | solution.py:301
  22.1 7.3 %collective-permute-start.5 = (f32[264,128]{1,0:T(8,128)S(1)}, f32[264,128]{1,0:T(8,128)S(1)}, u32[]{:S(2)}, u32[]{:S(2)}) collective-permute-start(f32[264,128]{1,0:T(8,128)S(1)} %get-tuple-element.100.refs_0_), channel_id=1, source_target_pairs={{0,32},{4,36},{8,40},{12,44},{16,48},{20,52},{24,56},{28,60},{32,6... | collective-permute-start | bytes 405512 | tf_op jit(solution)/shard_map/ppermute | solution.py:301
  22.5 7.0 %collective-permute-start.6 = (f32[264,128]{1,0:T(8,128)S(1)}, f32[264,128]{1,0:T(8,128)S(1)}, u32[]{:S(2)}, u32[]{:S(2)}) collective-permute-start(f32[264,128]{1,0:T(8,128)S(1)} %get-tuple-element.100.refs_0_), channel_id=1, source_target_pairs={{0,96},{4,100},{8,104},{12,108},{16,112},{20,116},{24,120},{28,124... | collective-permute-start | bytes 405512 | tf_op jit(solution)/shard_map/ppermute | solution.py:301
  29.7 6.2 %collective-permute-start.7 = (f32[256,128]{1,0:T(8,128)S(1)}, f32[256,128]{1,0:T(8,128)S(1)}, u32[]{:S(2)}, u32[]{:S(2)}) collective-permute-start(f32[256,128]{1,0:T(8,128)S(1)} %get-tuple-element.121), channel_id=1, source_target_pairs={{0,16},{4,20},{8,24},{12,28},{16,0},{20,4},{24,8},{28,12},{32,48},... | collective-permute-start | bytes 393224 | tf_op jit(solution)/shard_map/ppermute | solution.py:301
  30.1 8.3 %collective-permute-start.8 = (f32[256,128]{1,0:T(8,128)S(1)}, f32[256,128]{1,0:T(8,128)S(1)}, u32[]{:S(2)}, u32[]{:S(2)}) collective-permute-start(f32[256,128]{1,0:T(8,128)S(1)} %get-tuple-element.122), channel_id=1, source_target_pairs={{0,8},{4,12},{8,16},{12,20},{16,24},{20,28},{24,0},{28,4},{32,40},... | collective-permute-start | bytes 393224 | tf_op jit(solution)/shard_map/ppermute | solution.py:301
  31.1 7.3 %collective-permute-start.9 = (f32[256,128]{1,0:T(8,128)S(1)}, f32[256,128]{1,0:T(8,128)S(1)}, u32[]{:S(2)}, u32[]{:S(2)}) collective-permute-start(f32[256,128]{1,0:T(8,128)S(1)} %get-tuple-element.123), channel_id=1, source_target_pairs={{0,24},{4,28},{8,0},{12,4},{16,8},{20,12},{24,16},{28,20},{32,56},... | collective-permute-start | bytes 393224 | tf_op jit(solution)/shard_map/ppermute | solution.py:301
  35.9 4.5 %copy-start = (f32[2048]{0:T(1024)S(1)}, f32[2048]{0:T(1024)}, u32[]{:S(2)}) copy-start(f32[2048]{0:T(1024)} %param.10) | copy-start | bytes 24580
  38.5 3.6 %collective-permute-start.10 = (f32[4,256,128]{2,1,0:T(8,128)S(1)}, f32[4,256,128]{2,1,0:T(8,128)S(1)}, u32[]{:S(2)}, u32[]{:S(2)}) collective-permute-start(f32[4,256,128]{2,1,0:T(8,128)S(1)} %get-tuple-element.124), channel_id=1, source_target_pairs={{0,4},{4,0},{8,12},{12,8},{16,20},{20,16},{24,28},{28,24},{32,36},... | collective-permute-start | bytes 1572872 | tf_op jit(solution)/shard_map/ppermute | solution.py:322
  44.5 5.6 %collective-permute-start.11 = (f32[2,768]{1,0:T(2,128)S(1)}, f32[2,768]{1,0:T(2,128)S(1)}, u32[]{:S(2)}, u32[]{:S(2)}) collective-permute-start(f32[2,768]{1,0:T(2,128)S(1)} %get-tuple-element.131.refs_0_), channel_id=1, source_target_pairs={{0,2},{1,3},{2,0},{3,1},{4,6},{5,7},{6,4},{7,5},{8,10},{9,11},{10,... | collective-permute-start | bytes 18440 | tf_op jit(solution)/shard_map/ppermute | solution.py:802
  47.5 3.7 %collective-permute-start.12 = (f32[2,768]{1,0:T(2,128)S(1)}, f32[2,768]{1,0:T(2,128)S(1)}, u32[]{:S(2)}, u32[]{:S(2)}) collective-permute-start(f32[2,768]{1,0:T(2,128)S(1)} %get-tuple-element.131.refs_0_), channel_id=1, source_target_pairs={{0,1},{1,2},{2,3},{3,0},{4,5},{5,6},{6,7},{7,4},{8,9},{9,10},{10,1... | collective-permute-start | bytes 18440 | tf_op jit(solution)/shard_map/ppermute | solution.py:802
  47.9 3.3 %collective-permute-start.13 = (f32[2,768]{1,0:T(2,128)S(1)}, f32[2,768]{1,0:T(2,128)S(1)}, u32[]{:S(2)}, u32[]{:S(2)}) collective-permute-start(f32[2,768]{1,0:T(2,128)S(1)} %get-tuple-element.131.refs_0_), channel_id=1, source_target_pairs={{0,3},{1,0},{2,1},{3,2},{4,7},{5,4},{6,5},{7,6},{8,11},{9,8},{10,9... | collective-permute-start | bytes 18440 | tf_op jit(solution)/shard_map/ppermute | solution.py:802
  53.0 3.5 %collective-permute-start.14 = (f32[4,264,128]{2,1,0:T(8,128)S(1)}, f32[4,264,128]{2,1,0:T(8,128)S(1)}, u32[]{:S(2)}, u32[]{:S(2)}) collective-permute-start(f32[4,264,128]{2,1,0:T(8,128)S(1)} %get-tuple-element.136), channel_id=1, source_target_pairs={{0,4},{4,0},{8,12},{12,8},{16,20},{20,16},{24,28},{28,24},{32,36},... | collective-permute-start | bytes 1622024 | tf_op jit(solution)/shard_map/ppermute | solution.py:303
  56.6 9.0 %collective-permute-start.15 = (f32[264,128]{1,0:T(8,128)S(1)}, f32[264,128]{1,0:T(8,128)S(1)}, u32[]{:S(2)}, u32[]{:S(2)}) collective-permute-start(f32[264,128]{1,0:T(8,128)S(1)} %get-tuple-element.138), channel_id=1, source_target_pairs={{0,16},{4,20},{8,24},{12,28},{16,0},{20,4},{24,8},{28,12},{32,48},... | collective-permute-start | bytes 405512 | tf_op jit(solution)/shard_map/ppermute | solution.py:301
  57.2 9.5 %collective-permute-start.16 = (f32[264,128]{1,0:T(8,128)S(1)}, f32[264,128]{1,0:T(8,128)S(1)}, u32[]{:S(2)}, u32[]{:S(2)}) collective-permute-start(f32[264,128]{1,0:T(8,128)S(1)} %get-tuple-element.139), channel_id=1, source_target_pairs={{0,8},{4,12},{8,16},{12,20},{16,24},{20,28},{24,0},{28,4},{32,40},... | collective-permute-start | bytes 405512 | tf_op jit(solution)/shard_map/ppermute | solution.py:301
  58.6 8.0 %collective-permute-start.17 = (f32[264,128]{1,0:T(8,128)S(1)}, f32[264,128]{1,0:T(8,128)S(1)}, u32[]{:S(2)}, u32[]{:S(2)}) collective-permute-start(f32[264,128]{1,0:T(8,128)S(1)} %get-tuple-element.140), channel_id=1, source_target_pairs={{0,24},{4,28},{8,0},{12,4},{16,8},{20,12},{24,16},{28,20},{32,56},... | collective-permute-start | bytes 405512 | tf_op jit(solution)/shard_map/ppermute | solution.py:301
  66.7 9.2 %collective-permute-start.18 = (f32[264,128]{1,0:T(8,128)S(1)}, f32[264,128]{1,0:T(8,128)S(1)}, u32[]{:S(2)}, u32[]{:S(2)}) collective-permute-start(f32[264,128]{1,0:T(8,128)S(1)} %get-tuple-element.148.refs_0_), channel_id=1, source_target_pairs={{0,64},{4,68},{8,72},{12,76},{16,80},{20,84},{24,88},{28,92},{32,9... | collective-permute-start | bytes 405512 | tf_op jit(solution)/shard_map/ppermute | solution.py:301
  67.4 9.3 %collective-permute-start.19 = (f32[264,128]{1,0:T(8,128)S(1)}, f32[264,128]{1,0:T(8,128)S(1)}, u32[]{:S(2)}, u32[]{:S(2)}) collective-permute-start(f32[264,128]{1,0:T(8,128)S(1)} %get-tuple-element.148.refs_0_), channel_id=1, source_target_pairs={{0,32},{4,36},{8,40},{12,44},{16,48},{20,52},{24,56},{28,60},{32,6... | collective-permute-start | bytes 405512 | tf_op jit(solution)/shard_map/ppermute | solution.py:301
  69.2 7.6 %collective-permute-start.20 = (f32[264,128]{1,0:T(8,128)S(1)}, f32[264,128]{1,0:T(8,128)S(1)}, u32[]{:S(2)}, u32[]{:S(2)}) collective-permute-start(f32[264,128]{1,0:T(8,128)S(1)} %get-tuple-element.148.refs_0_), channel_id=1, source_target_pairs={{0,96},{4,100},{8,104},{12,108},{16,112},{20,116},{24,120},{28,124... | collective-permute-start | bytes 405512 | tf_op jit(solution)/shard_map/ppermute | solution.py:301
  76.9 7.3 %collective-permute-start.21 = (f32[264,128]{1,0:T(8,128)S(1)}, f32[264,128]{1,0:T(8,128)S(1)}, u32[]{:S(2)}, u32[]{:S(2)}) collective-permute-start(f32[264,128]{1,0:T(8,128)S(1)} %get-tuple-element.162), channel_id=1, source_target_pairs={{0,16},{4,20},{8,24},{12,28},{16,0},{20,4},{24,8},{28,12},{32,48},... | collective-permute-start | bytes 405512 | tf_op jit(solution)/shard_map/ppermute | solution.py:301
  77.3 9.6 %collective-permute-start.22 = (f32[264,128]{1,0:T(8,128)S(1)}, f32[264,128]{1,0:T(8,128)S(1)}, u32[]{:S(2)}, u32[]{:S(2)}) collective-permute-start(f32[264,128]{1,0:T(8,128)S(1)} %get-tuple-element.163), channel_id=1, source_target_pairs={{0,8},{4,12},{8,16},{12,20},{16,24},{20,28},{24,0},{28,4},{32,40},... | collective-permute-start | bytes 405512 | tf_op jit(solution)/shard_map/ppermute | solution.py:301
  78.8 8.1 %collective-permute-start.23 = (f32[264,128]{1,0:T(8,128)S(1)}, f32[264,128]{1,0:T(8,128)S(1)}, u32[]{:S(2)}, u32[]{:S(2)}) collective-permute-start(f32[264,128]{1,0:T(8,128)S(1)} %get-tuple-element.164), channel_id=1, source_target_pairs={{0,24},{4,28},{8,0},{12,4},{16,8},{20,12},{24,16},{28,20},{32,56},... | collective-permute-start | bytes 405512 | tf_op jit(solution)/shard_map/ppermute | solution.py:301
  87.0 2.4 %collective-permute-start.24 = (f32[4,264,128]{2,1,0:T(8,128)S(1)}, f32[4,264,128]{2,1,0:T(8,128)S(1)}, u32[]{:S(2)}, u32[]{:S(2)}) collective-permute-start(f32[4,264,128]{2,1,0:T(8,128)S(1)} %get-tuple-element.165), channel_id=1, source_target_pairs={{0,4},{4,0},{8,12},{12,8},{16,20},{20,16},{24,28},{28,24},{32,36},... | collective-permute-start | bytes 1622024 | tf_op jit(solution)/shard_map/ppermute | solution.py:322
where the time goes:
time: 93.9 us; the launch traced here: 93.8 us
  Pallas kernels  48.4 us (52%)
  starting transfers between devices  35.9 us (38%)
  waiting for transfers between devices  8.4 us (9%)
  between operations  1.05 us (1%)
    ppermute x18, starting transfers between devices, shifted(): lax.ppermute(arrays[s], 'seq', moves[s])  24.7 us
    pallas_call x3, Pallas kernels, grads_local(): pl.pallas_call(functools.partial(grads_body, first, count, bool(done)), i...  15.8 us
    pallas_call x3, Pallas kernels, attend(): pl.pallas_call(functools.partial(attend_body, first, count, load), in_spe...  13.8 us
    ppermute x18, waiting for transfers between devices, shifted(): lax.ppermute(arrays[s], 'seq', moves[s])  7.01 us
    pallas_call x2, Pallas kernels, grads_leaving(): pl.pallas_call(functools.partial(leave_body, of_other), in_specs=[VMEM] *...  6.03 us
    ppermute x3, starting transfers between devices, per_device(): lax.ppermute(stats, 'head', [(i, (i + s) % count) for i in range(count)])  5.62 us
    pallas_call x2, Pallas kernels, attend_entering(): pl.pallas_call(functools.partial(enter_body, of_other), in_specs=[VMEM] *...  4.13 us
    pallas_call x2, Pallas kernels, local_state(): pl.pallas_call(functools.partial(state_body, of_other), in_specs=specs, o...  4.13 us
  transfers between devices with their start and end apart: 25, of which 6 were waited for; matrix products, arithmetic and copies ran while one was open for 0% of the time, Pallas kernels for 38%

commit v1 on v0

--- a/solution.py
+++ b/solution.py
@@ -44,6 +44,10 @@
 
 def cost(flops, nbytes):
     return pl.CostEstimate(flops=int(flops), bytes_accessed=int(nbytes), transcendentals=0)
+
+
+def side_by_side(count):
+    return 3 if count % 3 == 0 else PAIR
 
 
 def head_rows(ref, head):
@@ -425,9 +429,11 @@
         else:
             held.append(copy)
 
-    @pl.loop(0, count // PAIR)
+    size = side_by_side(count)
+
+    @pl.loop(0, count // size)
     def _(at):
-        heads = [first + at * PAIR + a for a in range(PAIR)]
+        heads = [first + at * size + a for a in range(size)]
         attend_heads(heads, q_ref, k_ref, v_ref, cum_ref, outs, both_masks, picks)
 
     for copy in held:
@@ -658,22 +664,24 @@
     both_masks = masks()
     picks = block_picks(inputs[0].shape[0] // SPAN)
 
+    size = side_by_side(count)
+
     def copies(at):
-        here, there = head_lanes(at * PAIR, PAIR), head_lanes(first + at * PAIR, PAIR)
+        here, there = head_lanes(at * size, size), head_lanes(first + at * size, size)
         return [
             pltpu.make_async_copy(out_ref.at[:, here], out_hbm.at[:, there], sems.at[0, at]),
             pltpu.make_async_copy(gq_ref.at[:, here], gq_hbm.at[:, there], sems.at[1, at]),
         ]
 
-    @pl.loop(0, count // PAIR)
+    @pl.loop(0, count // size)
     def _(at):
-        places = [at * PAIR + a for a in range(PAIR)]
+        places = [at * size + a for a in range(size)]
         heads = [first + p for p in places]
         grads_heads(heads, places, inputs, out_ref, gq_ref, lk_ref, lv_ref, both_masks, picks)
         for copy in copies(at):
             copy.start()
 
-    @pl.loop(0, count // PAIR)
+    @pl.loop(0, count // size)
     def _(at):
         for copy in copies(at):
             copy.wait()
@@ -692,7 +700,7 @@
         scratch_shapes=[
             pltpu.VMEM((rows, count * DH), BF16),
             pltpu.VMEM((rows, count * DH), BF16),
-            pltpu.SemaphoreType.DMA((2, count // PAIR)),
+            pltpu.SemaphoreType.DMA((2, count // side_by_side(count))),
         ],
         compiler_params=params(8),
         cost_estimate=cost(22 * rows * count * DH * DH, 24 * rows * count * DH),

time: 93.9 us -> 93.1 us (level)
  starting transfers between devices: 35.9 us -> 38.9 us
  waiting for transfers between devices: 8.4 us -> 6.17 us
  Pallas kernels: 48.4 us -> 46.9 us
    ppermute x18, waiting for transfers between devices: 7.01 us -> 4.78 us  [shifted(): lax.ppermute(arrays[s], 'seq', moves[s])]
    ppermute x18, starting transfers between devices: 24.7 us -> 26.2 us  [shifted(): lax.ppermute(arrays[s], 'seq', moves[s])]
    ppermute x2, starting transfers between devices: 2.42 us -> 3.81 us  [scan_over_seq(): return (keep, lax.ppermute(give, 'seq', across), done)]
  transfers between devices with their start and end apart: 25 -> 25, of which waited for: 6 -> 6; matrix products, arithmetic and copies ran while one was open for 0% -> 0% of each run, Pallas kernels for 38% -> 37%
where the time goes in v1:
time: 93.1 us; the launch traced here: 93 us
  Pallas kernels  46.9 us (50%)
  starting transfers between devices  38.9 us (42%)
  waiting for transfers between devices  6.17 us (7%)
  between operations  1.05 us (1%)
    ppermute x18, starting transfers between devices, shifted(): lax.ppermute(arrays[s], 'seq', moves[s])  26.2 us
    pallas_call x3, Pallas kernels, grads_local(): pl.pallas_call(functools.partial(grads_body, first, count, bool(done)), i...  15.1 us
    pallas_call x3, Pallas kernels, attend(): pl.pallas_call(functools.partial(attend_body, first, count, load), in_spe...  12.9 us
    pallas_call x2, Pallas kernels, grads_leaving(): pl.pallas_call(functools.partial(leave_body, of_other), in_specs=[VMEM] *...  6.03 us
    ppermute x3, starting transfers between devices, per_device(): lax.ppermute(stats, 'head', [(i, (i + s) % count) for i in range(count)])  5.63 us
    ppermute x18, waiting for transfers between devices, shifted(): lax.ppermute(arrays[s], 'seq', moves[s])  4.78 us
    pallas_call x2, Pallas kernels, attend_entering(): pl.pallas_call(functools.partial(enter_body, of_other), in_specs=[VMEM] *...  4.13 us
    pallas_call x2, Pallas kernels, local_state(): pl.pallas_call(functools.partial(state_body, of_other), in_specs=specs, o...  4.13 us
  transfers between devices with their start and end apart: 25, of which 6 were waited for; matrix products, arithmetic and copies ran while one was open for 0% of the time, Pallas kernels for 37%

profile of v1, /device:TPU:1, one launch (start us, length us, event | category | flops | bytes accessed | tf_op | source)
XLA Modules:
  0.0 93.0 jit_solution(13573178929297055218)
XLA Ops:
  0.6 2.9 %state_given.1 = (f32[4,264,128]{2,1,0:T(8,128)S(1)}, bf16[768,2048]{1,0:T(8,128)(2,1)S(1)}, bf16[768,2048]{1,0:T(8,128)(2,1)S(1)}, f32[128,128]{1,0:T(8,128)S(1...) custom-call(bf16[768,2048]{1,0:T(8,128)(2,1)} %refs_0_.1, bf16[768,2048]{1,0:T(8,128)(2,1)} %refs_1_.1, f32[16,768]{1,0:T(8,128)} %refs_2_.1), custom_call_target="tpu_custom_call" | custom-call | flops 201326592 | bytes 3145728 | tf_op jit(solution)/shard_map/state_given/pallas_call | solution.py:187
  3.6 1.5 %collective-permute-start = (f32[4,264,128]{2,1,0:T(8,128)S(1)}, f32[4,264,128]{2,1,0:T(8,128)S(1)}, u32[]{:S(2)}, u32[]{:S(2)}) collective-permute-start(f32[4,264,128]{2,1,0:T(8,128)S(1)} %get-tuple-element.94), channel_id=1, source_target_pairs={{0,4},{4,0},{8,12},{12,8},{16,20},{20,16},{24,28},{28,24},{32,36},... | collective-permute-start | bytes 1622024 | tf_op jit(solution)/shard_map/ppermute | solution.py:307
  5.1 1.2 %state_kept.1.own_ref.refs_4_ = f32[4,264,128]{2,1,0:T(8,128)S(1)} custom-call(bf16[768,2048]{1,0:T(8,128)(2,1)S(1)} %get-tuple-element.89.refs_0_.refs_1_.refs_2_, bf16[768,2048]{1,0:T(8,128)(2,1)S(1)} %get-tuple-element.90.refs_1_.refs_2_, f32[128,128]{1,0:T(8,128)S(1)} %get-tuple-element.91.refs_2_.refs_3_.cum_ref.refs_13_, ...), custom_call_target="tpu_custom_call" | custom-call | flops 201326592 | bytes 3145728 | tf_op jit(solution)/shard_map/state_kept/pallas_call | solution.py:187
  6.3 0.4 collective-permute-done.got_ref.refs_5_
  6.7 3.8 %collective-permute-start.1 = (f32[264,128]{1,0:T(8,128)S(1)}, f32[264,128]{1,0:T(8,128)S(1)}, u32[]{:S(2)}, u32[]{:S(2)}) collective-permute-start(f32[264,128]{1,0:T(8,128)S(1)} %get-tuple-element.96), channel_id=1, source_target_pairs={{0,16},{4,20},{8,24},{12,28},{16,0},{20,4},{24,8},{28,12},{32,48},... | collective-permute-start | bytes 405512 | tf_op jit(solution)/shard_map/ppermute | solution.py:305
  10.5 0.7 collective-permute-start.2
  11.2 1.9 %collective-permute-start.3 = (f32[264,128]{1,0:T(8,128)S(1)}, f32[264,128]{1,0:T(8,128)S(1)}, u32[]{:S(2)}, u32[]{:S(2)}) collective-permute-start(f32[264,128]{1,0:T(8,128)S(1)} %get-tuple-element.98), channel_id=1, source_target_pairs={{0,24},{4,28},{8,0},{12,4},{16,8},{20,12},{24,16},{28,20},{32,56},... | collective-permute-start | bytes 405512 | tf_op jit(solution)/shard_map/ppermute | solution.py:305
  13.2 5.6 %attend_0.1 = (bf16[768,2048]{1,0:T(8,128)(2,1)S(1)}, bf16[16,6,128,128]{3,2,1,0:T(8,128)(2,1)S(1)}, bf16[16,128,768]{2,1,0:T(8,128)(2,1)S(1)}, bf16[768,2048]{1...) custom-call(f32[264,128]{1,0:T(8,128)S(1)} %get-tuple-element.95.ref, ...), custom_call_target="tpu_custom_call" | custom-call | flops 754974720 | bytes 7077888 | tf_op jit(solution)/shard_map/attend_0/pallas_call | solution.py:457
  18.9 2.8 %collective-permute-start.4 = (f32[264,128]{1,0:T(8,128)S(1)}, f32[264,128]{1,0:T(8,128)S(1)}, u32[]{:S(2)}, u32[]{:S(2)}) collective-permute-start(f32[264,128]{1,0:T(8,128)S(1)} %get-tuple-element.100.refs_0_), channel_id=1, source_target_pairs={{0,64},{4,68},{8,72},{12,76},{16,80},{20,84},{24,88},{28,92},{32,9... | collective-permute-start | bytes 405512 | tf_op jit(solution)/shard_map/ppermute | solution.py:305
  21.7 0.3 collective-permute-start.5
  22.0 2.4 %collective-permute-start.6 = (f32[264,128]{1,0:T(8,128)S(1)}, f32[264,128]{1,0:T(8,128)S(1)}, u32[]{:S(2)}, u32[]{:S(2)}) collective-permute-start(f32[264,128]{1,0:T(8,128)S(1)} %get-tuple-element.100.refs_0_), channel_id=1, source_target_pairs={{0,96},{4,100},{8,104},{12,108},{16,112},{20,116},{24,120},{28,124... | collective-permute-start | bytes 405512 | tf_op jit(solution)/shard_map/ppermute | solution.py:305
  24.4 4.2 %attend_6.1 = (bf16[768,2048]{1,0:T(8,128)(2,1)S(1)}, bf16[16,6,128,128]{3,2,1,0:T(8,128)(2,1)S(1)}, bf16[16,128,768]{2,1,0:T(8,128)(2,1)S(1)}, bf16[768,2048]{1...) custom-call(f32[264,128]{1,0:T(8,128)S(1)} %get-tuple-element.100.re, ...), custom_call_target="tpu_custom_call", output_to_operand_aliasing={{0}: (6, {}), {1}: (7, {}), {2}: (8, {}), {3}: (9, {}), {4}... | custom-call | flops 754974720 | bytes 7077888 | tf_op jit(solution)/shard_map/attend_6/pallas_call | solution.py:457
  28.7 0.2 join_x.2
  28.8 0.8 collective-permute-start.7
  29.7 1.0 %collective-permute-start.8 = (f32[256,128]{1,0:T(8,128)S(1)}, f32[256,128]{1,0:T(8,128)S(1)}, u32[]{:S(2)}, u32[]{:S(2)}) collective-permute-start(f32[256,128]{1,0:T(8,128)S(1)} %get-tuple-element.122), channel_id=1, source_target_pairs={{0,8},{4,12},{8,16},{12,20},{16,24},{20,28},{24,0},{28,4},{32,40},... | collective-permute-start | bytes 393224 | tf_op jit(solution)/shard_map/ppermute | solution.py:305
  30.7 1.7 %collective-permute-start.9 = (f32[256,128]{1,0:T(8,128)S(1)}, f32[256,128]{1,0:T(8,128)S(1)}, u32[]{:S(2)}, u32[]{:S(2)}) collective-permute-start(f32[256,128]{1,0:T(8,128)S(1)} %get-tuple-element.123), channel_id=1, source_target_pairs={{0,24},{4,28},{8,0},{12,4},{16,8},{20,12},{24,16},{28,20},{32,56},... | collective-permute-start | bytes 393224 | tf_op jit(solution)/shard_map/ppermute | solution.py:305
  32.3 3.1 %attend_12.1 = (bf16[768,2048]{1,0:T(8,128)(2,1)S(1)}, bf16[16,6,128,128]{3,2,1,0:T(8,128)(2,1)S(1)}, bf16[16,128,768]{2,1,0:T(8,128)(2,1)S(1)}, bf16[768,2048]{...) custom-call(f32[256,128]{1,0:T(8,128)S(1)} %get-tuple-element.110.re, ...), custom_call_target="tpu_custom_call", output_to_operand_aliasing={{0}: (5, {}), {1}: (6, {}), {2}: (7, {}), {3}: (8, {}), {4}... | custom-call | flops 503316480 | bytes 4718592 | tf_op jit(solution)/shard_map/attend_12/pallas_call | solution.py:457
  35.5 0.7 collective-permute-done.8.refs_2_
  36.3 3.2 %collective-permute-start.10 = (f32[4,256,128]{2,1,0:T(8,128)S(1)}, f32[4,256,128]{2,1,0:T(8,128)S(1)}, u32[]{:S(2)}, u32[]{:S(2)}) collective-permute-start(f32[4,256,128]{2,1,0:T(8,128)S(1)} %get-tuple-element.124), channel_id=1, source_target_pairs={{0,4},{4,0},{8,12},{12,8},{16,20},{20,16},{24,28},{28,24},{32,36},... | collective-permute-start | bytes 1572872 | tf_op jit(solution)/shard_map/ppermute | solution.py:326
  39.5 1.7 %enter_kept.1 = (bf16[768,2048]{1,0:T(8,128)(2,1)S(1)}, bf16[16,128,128]{2,1,0:T(8,128)(2,1)S(1)}, f32[768,128]{1,0:T(8,128)S(1)}, f32[768,128]{1,0:T(8,128)S(1)}) custom-call(bf16[768,2048]{1,0:T(8,128)(2,1)S(1)} %get-tuple-element.118.q_ref, bf16[768,2048]{1,0:T(8,128)(2,1)S(1)} %get-tuple-element.119.refs_6_.local_ref, ...), custom_call_target="tpu_custom_call" | custom-call | flops 201326592 | bytes 6291456 | tf_op jit(solution)/shard_map/enter_kept/pallas_call | solution.py:520
  41.2 2.4 %enter_taken.1 = (bf16[768,2048]{1,0:T(8,128)(2,1)S(1)}, bf16[16,128,128]{2,1,0:T(8,128)(2,1)S(1)}, f32[2,768]{1,0:T(2,128)S(1)}, f32[768,128]{1,0:T(8,128)S(1)}, f32[768,128]{1,0:T(8,128)S(1)}) custom-call(bf16[768,2048]{1,0:T(8,128)(2,1)S(1)} %get-tuple-element.118.q_ref, ...), custom_call_target="tpu_custom_call", output_to_operand_aliasing={{0}: (7, {}), {1}: (8, {}), {3}: (9, {}), {4}: (10, {})} | custom-call | flops 201326592 | bytes 6291456 | tf_op jit(solution)/shard_map/enter_taken/pallas_call | solution.py:520
  43.7 3.0 %collective-permute-start.11 = (f32[2,768]{1,0:T(2,128)S(1)}, f32[2,768]{1,0:T(2,128)S(1)}, u32[]{:S(2)}, u32[]{:S(2)}) collective-permute-start(f32[2,768]{1,0:T(2,128)S(1)} %get-tuple-element.131.refs_0_), channel_id=1, source_target_pairs={{0,2},{1,3},{2,0},{3,1},{4,6},{5,7},{6,4},{7,5},{8,10},{9,11},{10,... | collective-permute-start | bytes 18440 | tf_op jit(solution)/shard_map/ppermute | solution.py:810
  46.6 0.4 collective-permute-start.12
  47.0 2.3 %collective-permute-start.13 = (f32[2,768]{1,0:T(2,128)S(1)}, f32[2,768]{1,0:T(2,128)S(1)}, u32[]{:S(2)}, u32[]{:S(2)}) collective-permute-start(f32[2,768]{1,0:T(2,128)S(1)} %get-tuple-element.131.refs_0_), channel_id=1, source_target_pairs={{0,3},{1,0},{2,1},{3,2},{4,7},{5,4},{6,5},{7,6},{8,11},{9,8},{10,9... | collective-permute-start | bytes 18440 | tf_op jit(solution)/shard_map/ppermute | solution.py:810
  49.3 1.0 %collective-permute-done.12.refs_2_ = f32[2,768]{1,0:T(2,128)S(1)} collective-permute-done((f32[2,768]{1,0:T(2,128)S(1)}, f32[2,768]{1,0:T(2,128)S(1)}, u32[]{:S(2)}, u32[]{:S(2)}) %collective-permute-start.12) | collective-permute-done | bytes 6176 | tf_op jit(solution)/shard_map/ppermute | solution.py:810
  50.3 1.9 %norm_given.1 = (bf16[768,2048]{1,0:T(8,128)(2,1)S(1)}, f32[4,264,128]{2,1,0:T(8,128)S(1)}, f32[768,128]{1,0:T(8,128)S(1)}, f32[768,128]{1,0:T(8,128)S(1)}) custom-call(bf16[16,128,768]{2,1,0:T(8,128)(2,1)S(1)} %get-tuple-element.117.turned_ref.refs_3_, bf16[768,2048]{1,0:T(8,128)(2,1)S(1)} %get-tuple-element.130.attn_ref.refs_8_, ...), custom_call_target="tpu_custom_call" | custom-call | flops 201326592 | bytes 6291456 | tf_op jit(solution)/shard_map/norm_given/pallas_call | solution.py:581
  52.2 1.7 %collective-permute-start.14 = (f32[4,264,128]{2,1,0:T(8,128)S(1)}, f32[4,264,128]{2,1,0:T(8,128)S(1)}, u32[]{:S(2)}, u32[]{:S(2)}) collective-permute-start(f32[4,264,128]{2,1,0:T(8,128)S(1)} %get-tuple-element.136), channel_id=1, source_target_pairs={{0,4},{4,0},{8,12},{12,8},{16,20},{20,16},{24,28},{28,24},{32,36},... | collective-permute-start | bytes 1622024 | tf_op jit(solution)/shard_map/ppermute | solution.py:307
  53.9 1.8 %norm_kept.1 = (bf16[768,2048]{1,0:T(8,128)(2,1)S(1)}, f32[4,264,128]{2,1,0:T(8,128)S(1)}) custom-call(bf16[16,128,768]{2,1,0:T(8,128)(2,1)S(1)} %get-tuple-element.117.turned_ref.refs_3_, bf16[768,2048]{1,0:T(8,128)(2,1)S(1)} %get-tuple-element.130.attn_ref.refs_8_, ...), custom_call_target="tpu_custom_call", output_to_operand_aliasing={{0}: (9, {})} | custom-call | flops 201326592 | bytes 6291456 | tf_op jit(solution)/shard_map/norm_kept/pallas_call | solution.py:581
  55.8 0.8 collective-permute-start.15
  56.6 1.6 %collective-permute-start.16 = (f32[264,128]{1,0:T(8,128)S(1)}, f32[264,128]{1,0:T(8,128)S(1)}, u32[]{:S(2)}, u32[]{:S(2)}) collective-permute-start(f32[264,128]{1,0:T(8,128)S(1)} %get-tuple-element.139), channel_id=1, source_target_pairs={{0,8},{4,12},{8,16},{12,20},{16,24},{20,28},{24,0},{28,4},{32,40},... | collective-permute-start | bytes 405512 | tf_op jit(solution)/shard_map/ppermute | solution.py:305
  58.2 1.1 %collective-permute-start.17 = (f32[264,128]{1,0:T(8,128)S(1)}, f32[264,128]{1,0:T(8,128)S(1)}, u32[]{:S(2)}, u32[]{:S(2)}) collective-permute-start(f32[264,128]{1,0:T(8,128)S(1)} %get-tuple-element.140), channel_id=1, source_target_pairs={{0,24},{4,28},{8,0},{12,4},{16,8},{20,12},{24,16},{28,20},{32,56},... | collective-permute-start | bytes 405512 | tf_op jit(solution)/shard_map/ppermute | solution.py:305
  59.3 5.4 %grads_0.1 = (bf16[768,2048]{1,0:T(8,128)(2,1)}, bf16[768,2048]{1,0:T(8,128)(2,1)}, bf16[768,2048]{1,0:T(8,128)(2,1)S(1)}, bf16[768,2048]{1,0:T(8,128)(2,1)S(1)}) custom-call(f32[264,128]{1,0:T(8,128)S(1)} %get-tuple-element.137.refs_0_, bf16[768,2048]{1,0:T(8,128)(2,1)S(1)} %get-tuple-element.102.refs_4_.refs_1_, ...), custom_call_target="tpu_custom_call" | custom-call | flops 1660944384 | bytes 14155776 | tf_op jit(solution)/shard_map/grads_0/pallas_call | solution.py:694
  64.8 1.0 %collective-permute-done.16.refs_2_ = f32[264,128]{1,0:T(8,128)S(1)} collective-permute-done((f32[264,128]{1,0:T(8,128)S(1)}, f32[264,128]{1,0:T(8,128)S(1)}, u32[]{:S(2)}, u32[]{:S(2)}) %collective-permute-start.16) | collective-permute-done | bytes 135200 | tf_op jit(solution)/shard_map/ppermute | solution.py:305
  65.9 1.1 %collective-permute-start.18 = (f32[264,128]{1,0:T(8,128)S(1)}, f32[264,128]{1,0:T(8,128)S(1)}, u32[]{:S(2)}, u32[]{:S(2)}) collective-permute-start(f32[264,128]{1,0:T(8,128)S(1)} %get-tuple-element.148.refs_0_), channel_id=1, source_target_pairs={{0,64},{4,68},{8,72},{12,76},{16,80},{20,84},{24,88},{28,92},{32,9... | collective-permute-start | bytes 405512 | tf_op jit(solution)/shard_map/ppermute | solution.py:305
  67.1 1.7 %collective-permute-start.19 = (f32[264,128]{1,0:T(8,128)S(1)}, f32[264,128]{1,0:T(8,128)S(1)}, u32[]{:S(2)}, u32[]{:S(2)}) collective-permute-start(f32[264,128]{1,0:T(8,128)S(1)} %get-tuple-element.148.refs_0_), channel_id=1, source_target_pairs={{0,32},{4,36},{8,40},{12,44},{16,48},{20,52},{24,56},{28,60},{32,6... | collective-permute-start | bytes 405512 | tf_op jit(solution)/shard_map/ppermute | solution.py:305
  68.7 1.0 %collective-permute-start.20 = (f32[264,128]{1,0:T(8,128)S(1)}, f32[264,128]{1,0:T(8,128)S(1)}, u32[]{:S(2)}, u32[]{:S(2)}) collective-permute-start(f32[264,128]{1,0:T(8,128)S(1)} %get-tuple-element.148.refs_0_), channel_id=1, source_target_pairs={{0,96},{4,100},{8,104},{12,108},{16,112},{20,116},{24,120},{28,124... | collective-permute-start | bytes 405512 | tf_op jit(solution)/shard_map/ppermute | solution.py:305
  69.7 5.5 %grads_6.1 = (bf16[768,2048]{1,0:T(8,128)(2,1)}, bf16[768,2048]{1,0:T(8,128)(2,1)}, bf16[768,2048]{1,0:T(8,128)(2,1)S(1)}, bf16[768,2048]{1,0:T(8,128)(2,1)S(1)}) custom-call(f32[264,128]{1,0:T(8,128)S(1)} %get-tuple-element.148.refs_0_, ...), custom_call_target="tpu_custom_call", output_to_operand_aliasing={{0}: (15, {}), {1}: (16, {}), {2}: (17, {}), {3}: (18, {})} | custom-call | flops 1660944384 | bytes 14155776 | tf_op jit(solution)/shard_map/grads_6/pallas_call | solution.py:694
  75.2 0.7 collective-permute-done.19.refs_2_
  75.9 0.2 join_x.3
  76.1 0.8 collective-permute-start.21
  76.9 1.5 %collective-permute-start.22 = (f32[264,128]{1,0:T(8,128)S(1)}, f32[264,128]{1,0:T(8,128)S(1)}, u32[]{:S(2)}, u32[]{:S(2)}) collective-permute-start(f32[264,128]{1,0:T(8,128)S(1)} %get-tuple-element.163), channel_id=1, source_target_pairs={{0,8},{4,12},{8,16},{12,20},{16,24},{20,28},{24,0},{28,4},{32,40},... | collective-permute-start | bytes 405512 | tf_op jit(solution)/shard_map/ppermute | solution.py:305
  78.4 1.2 %collective-permute-start.23 = (f32[264,128]{1,0:T(8,128)S(1)}, f32[264,128]{1,0:T(8,128)S(1)}, u32[]{:S(2)}, u32[]{:S(2)}) collective-permute-start(f32[264,128]{1,0:T(8,128)S(1)} %get-tuple-element.164), channel_id=1, source_target_pairs={{0,24},{4,28},{8,0},{12,4},{16,8},{20,12},{24,16},{28,20},{32,56},... | collective-permute-start | bytes 405512 | tf_op jit(solution)/shard_map/ppermute | solution.py:305
  79.6 4.2 %grads_12.1 = (bf16[768,2048]{1,0:T(8,128)(2,1)}, bf16[768,2048]{1,0:T(8,128)(2,1)}, bf16[768,2048]{1,0:T(8,128)(2,1)S(1)}, bf16[768,2048]{1,0:T(8,128)(2,1)S(1)}) custom-call(f32[264,128]{1,0:T(8,128)S(1)} %get-tuple-element.154.refs_0_, ...), custom_call_target="tpu_custom_call", output_to_operand_aliasing={{0}: (15, {}), {1}: (16, {}), {2}: (17, {}), {3}: (18, {})} | custom-call | flops 1107296256 | bytes 9437184 | tf_op jit(solution)/shard_map/grads_12/pallas_call | solution.py:694
  83.7 2.3 %collective-permute-done.22.refs_2_ = f32[264,128]{1,0:T(8,128)S(1)} collective-permute-done((f32[264,128]{1,0:T(8,128)S(1)}, f32[264,128]{1,0:T(8,128)S(1)}, u32[]{:S(2)}, u32[]{:S(2)}) %collective-permute-start.22) | collective-permute-done | bytes 135200 | tf_op jit(solution)/shard_map/ppermute | solution.py:305
  86.1 0.1 entering.3
  86.2 0.6 collective-permute-start.24
  86.8 1.8 %leave_kept.1 = (bf16[768,1024]{1,0:T(8,128)(2,1)S(1)}, bf16[768,1024]{1,0:T(8,128)(2,1)S(1)}, f32[1,2048]{1,0:T(1,128)S(1)}) custom-call(bf16[768,2048]{1,0:T(8,128)(2,1)S(1)} %get-tuple-element.141.refs_4_.k_ref, bf16[768,2048]{1,0:T(8,128)(2,1)S(1)} %get-tuple-element.142.refs_5_.v_ref, bf16[768,2048]{1,0:T(8,128)(2,1)S(1)} %get-tuple-element.160.lk_ref, ...), custom_call_target="tpu_custom_call" | custom-call | flops 402653184 | bytes 9437184 | tf_op jit(solution)/shard_map/leave_kept/pallas_call | solution.py:770
  88.6 4.2 %leave_taken.1 = (bf16[768,2048]{1,0:T(8,128)(2,1)}, bf16[768,2048]{1,0:T(8,128)(2,1)}, f32[1,2048]{1,0:T(1,128)}) custom-call(bf16[768,2048]{1,0:T(8,128)(2,1)S(1)} %get-tuple-element.141.refs_4_.k_ref, bf16[768,2048]{1,0:T(8,128)(2,1)S(1)} %get-tuple-element.142.refs_5_.v_ref, bf16[768,2048]{1,0:T(8,128)(2,1)S(1)} %get-tuple-element.160.lk_ref, ...), custom_call_target="tpu_custom_call" | custom-call | flops 402653184 | bytes 9437184 | tf_op jit(solution)/shard_map/leave_taken/pallas_call | solution.py:770
  (26 shorter events, 0.6 us)
Async XLA Ops:
  3.6 3.1 %collective-permute-start = (f32[4,264,128]{2,1,0:T(8,128)S(1)}, f32[4,264,128]{2,1,0:T(8,128)S(1)}, u32[]{:S(2)}, u32[]{:S(2)}) collective-permute-start(f32[4,264,128]{2,1,0:T(8,128)S(1)} %get-tuple-element.94), channel_id=1, source_target_pairs={{0,4},{4,0},{8,12},{12,8},{16,20},{20,16},{24,28},{28,24},{32,36},... | collective-permute-start | bytes 1622024 | tf_op jit(solution)/shard_map/ppermute | solution.py:307
  6.7 12.0 %collective-permute-start.1 = (f32[264,128]{1,0:T(8,128)S(1)}, f32[264,128]{1,0:T(8,128)S(1)}, u32[]{:S(2)}, u32[]{:S(2)}) collective-permute-start(f32[264,128]{1,0:T(8,128)S(1)} %get-tuple-element.96), channel_id=1, source_target_pairs={{0,16},{4,20},{8,24},{12,28},{16,0},{20,4},{24,8},{28,12},{32,48},... | collective-permute-start | bytes 405512 | tf_op jit(solution)/shard_map/ppermute | solution.py:305
  10.5 8.3 %collective-permute-start.2 = (f32[264,128]{1,0:T(8,128)S(1)}, f32[264,128]{1,0:T(8,128)S(1)}, u32[]{:S(2)}, u32[]{:S(2)}) collective-permute-start(f32[264,128]{1,0:T(8,128)S(1)} %get-tuple-element.97), channel_id=1, source_target_pairs={{0,8},{4,12},{8,16},{12,20},{16,24},{20,28},{24,0},{28,4},{32,40},... | collective-permute-start | bytes 405512 | tf_op jit(solution)/shard_map/ppermute | solution.py:305
  11.2 7.6 %collective-permute-start.3 = (f32[264,128]{1,0:T(8,128)S(1)}, f32[264,128]{1,0:T(8,128)S(1)}, u32[]{:S(2)}, u32[]{:S(2)}) collective-permute-start(f32[264,128]{1,0:T(8,128)S(1)} %get-tuple-element.98), channel_id=1, source_target_pairs={{0,24},{4,28},{8,0},{12,4},{16,8},{20,12},{24,16},{28,20},{32,56},... | collective-permute-start | bytes 405512 | tf_op jit(solution)/shard_map/ppermute | solution.py:305
  18.9 9.7 %collective-permute-start.4 = (f32[264,128]{1,0:T(8,128)S(1)}, f32[264,128]{1,0:T(8,128)S(1)}, u32[]{:S(2)}, u32[]{:S(2)}) collective-permute-start(f32[264,128]{1,0:T(8,128)S(1)} %get-tuple-element.100.refs_0_), channel_id=1, source_target_pairs={{0,64},{4,68},{8,72},{12,76},{16,80},{20,84},{24,88},{28,92},{32,9... | collective-permute-start | bytes 405512 | tf_op jit(solution)/shard_map/ppermute | solution.py:305
  21.7 6.9 %collective-permute-start.5 = (f32[264,128]{1,0:T(8,128)S(1)}, f32[264,128]{1,0:T(8,128)S(1)}, u32[]{:S(2)}, u32[]{:S(2)}) collective-permute-start(f32[264,128]{1,0:T(8,128)S(1)} %get-tuple-element.100.refs_0_), channel_id=1, source_target_pairs={{0,32},{4,36},{8,40},{12,44},{16,48},{20,52},{24,56},{28,60},{32,6... | collective-permute-start | bytes 405512 | tf_op jit(solution)/shard_map/ppermute | solution.py:305
  22.0 6.6 %collective-permute-start.6 = (f32[264,128]{1,0:T(8,128)S(1)}, f32[264,128]{1,0:T(8,128)S(1)}, u32[]{:S(2)}, u32[]{:S(2)}) collective-permute-start(f32[264,128]{1,0:T(8,128)S(1)} %get-tuple-element.100.refs_0_), channel_id=1, source_target_pairs={{0,96},{4,100},{8,104},{12,108},{16,112},{20,116},{24,120},{28,124... | collective-permute-start | bytes 405512 | tf_op jit(solution)/shard_map/ppermute | solution.py:305
  28.8 6.6 %collective-permute-start.7 = (f32[256,128]{1,0:T(8,128)S(1)}, f32[256,128]{1,0:T(8,128)S(1)}, u32[]{:S(2)}, u32[]{:S(2)}) collective-permute-start(f32[256,128]{1,0:T(8,128)S(1)} %get-tuple-element.121), channel_id=1, source_target_pairs={{0,16},{4,20},{8,24},{12,28},{16,0},{20,4},{24,8},{28,12},{32,48},... | collective-permute-start | bytes 393224 | tf_op jit(solution)/shard_map/ppermute | solution.py:305
  29.7 6.5 %collective-permute-start.8 = (f32[256,128]{1,0:T(8,128)S(1)}, f32[256,128]{1,0:T(8,128)S(1)}, u32[]{:S(2)}, u32[]{:S(2)}) collective-permute-start(f32[256,128]{1,0:T(8,128)S(1)} %get-tuple-element.122), channel_id=1, source_target_pairs={{0,8},{4,12},{8,16},{12,20},{16,24},{20,28},{24,0},{28,4},{32,40},... | collective-permute-start | bytes 393224 | tf_op jit(solution)/shard_map/ppermute | solution.py:305
  30.7 5.5 %collective-permute-start.9 = (f32[256,128]{1,0:T(8,128)S(1)}, f32[256,128]{1,0:T(8,128)S(1)}, u32[]{:S(2)}, u32[]{:S(2)}) collective-permute-start(f32[256,128]{1,0:T(8,128)S(1)} %get-tuple-element.123), channel_id=1, source_target_pairs={{0,24},{4,28},{8,0},{12,4},{16,8},{20,12},{24,16},{28,20},{32,56},... | collective-permute-start | bytes 393224 | tf_op jit(solution)/shard_map/ppermute | solution.py:305
  35.5 4.1 %copy-start = (f32[2048]{0:T(1024)S(1)}, f32[2048]{0:T(1024)}, u32[]{:S(2)}) copy-start(f32[2048]{0:T(1024)} %param.10) | copy-start | bytes 24580
  36.3 4.9 %collective-permute-start.10 = (f32[4,256,128]{2,1,0:T(8,128)S(1)}, f32[4,256,128]{2,1,0:T(8,128)S(1)}, u32[]{:S(2)}, u32[]{:S(2)}) collective-permute-start(f32[4,256,128]{2,1,0:T(8,128)S(1)} %get-tuple-element.124), channel_id=1, source_target_pairs={{0,4},{4,0},{8,12},{12,8},{16,20},{20,16},{24,28},{28,24},{32,36},... | collective-permute-start | bytes 1572872 | tf_op jit(solution)/shard_map/ppermute | solution.py:326
  43.7 5.6 %collective-permute-start.11 = (f32[2,768]{1,0:T(2,128)S(1)}, f32[2,768]{1,0:T(2,128)S(1)}, u32[]{:S(2)}, u32[]{:S(2)}) collective-permute-start(f32[2,768]{1,0:T(2,128)S(1)} %get-tuple-element.131.refs_0_), channel_id=1, source_target_pairs={{0,2},{1,3},{2,0},{3,1},{4,6},{5,7},{6,4},{7,5},{8,10},{9,11},{10,... | collective-permute-start | bytes 18440 | tf_op jit(solution)/shard_map/ppermute | solution.py:810
  46.6 3.7 %collective-permute-start.12 = (f32[2,768]{1,0:T(2,128)S(1)}, f32[2,768]{1,0:T(2,128)S(1)}, u32[]{:S(2)}, u32[]{:S(2)}) collective-permute-start(f32[2,768]{1,0:T(2,128)S(1)} %get-tuple-element.131.refs_0_), channel_id=1, source_target_pairs={{0,1},{1,2},{2,3},{3,0},{4,5},{5,6},{6,7},{7,4},{8,9},{9,10},{10,1... | collective-permute-start | bytes 18440 | tf_op jit(solution)/shard_map/ppermute | solution.py:810
  47.0 3.3 %collective-permute-start.13 = (f32[2,768]{1,0:T(2,128)S(1)}, f32[2,768]{1,0:T(2,128)S(1)}, u32[]{:S(2)}, u32[]{:S(2)}) collective-permute-start(f32[2,768]{1,0:T(2,128)S(1)} %get-tuple-element.131.refs_0_), channel_id=1, source_target_pairs={{0,3},{1,0},{2,1},{3,2},{4,7},{5,4},{6,5},{7,6},{8,11},{9,8},{10,9... | collective-permute-start | bytes 18440 | tf_op jit(solution)/shard_map/ppermute | solution.py:810
  52.2 3.5 %collective-permute-start.14 = (f32[4,264,128]{2,1,0:T(8,128)S(1)}, f32[4,264,128]{2,1,0:T(8,128)S(1)}, u32[]{:S(2)}, u32[]{:S(2)}) collective-permute-start(f32[4,264,128]{2,1,0:T(8,128)S(1)} %get-tuple-element.136), channel_id=1, source_target_pairs={{0,4},{4,0},{8,12},{12,8},{16,20},{20,16},{24,28},{28,24},{32,36},... | collective-permute-start | bytes 1622024 | tf_op jit(solution)/shard_map/ppermute | solution.py:307
  55.8 8.9 %collective-permute-start.15 = (f32[264,128]{1,0:T(8,128)S(1)}, f32[264,128]{1,0:T(8,128)S(1)}, u32[]{:S(2)}, u32[]{:S(2)}) collective-permute-start(f32[264,128]{1,0:T(8,128)S(1)} %get-tuple-element.138), channel_id=1, source_target_pairs={{0,16},{4,20},{8,24},{12,28},{16,0},{20,4},{24,8},{28,12},{32,48},... | collective-permute-start | bytes 405512 | tf_op jit(solution)/shard_map/ppermute | solution.py:305
  56.6 9.2 %collective-permute-start.16 = (f32[264,128]{1,0:T(8,128)S(1)}, f32[264,128]{1,0:T(8,128)S(1)}, u32[]{:S(2)}, u32[]{:S(2)}) collective-permute-start(f32[264,128]{1,0:T(8,128)S(1)} %get-tuple-element.139), channel_id=1, source_target_pairs={{0,8},{4,12},{8,16},{12,20},{16,24},{20,28},{24,0},{28,4},{32,40},... | collective-permute-start | bytes 405512 | tf_op jit(solution)/shard_map/ppermute | solution.py:305
  58.2 7.6 %collective-permute-start.17 = (f32[264,128]{1,0:T(8,128)S(1)}, f32[264,128]{1,0:T(8,128)S(1)}, u32[]{:S(2)}, u32[]{:S(2)}) collective-permute-start(f32[264,128]{1,0:T(8,128)S(1)} %get-tuple-element.140), channel_id=1, source_target_pairs={{0,24},{4,28},{8,0},{12,4},{16,8},{20,12},{24,16},{28,20},{32,56},... | collective-permute-start | bytes 405512 | tf_op jit(solution)/shard_map/ppermute | solution.py:305
  65.9 9.3 %collective-permute-start.18 = (f32[264,128]{1,0:T(8,128)S(1)}, f32[264,128]{1,0:T(8,128)S(1)}, u32[]{:S(2)}, u32[]{:S(2)}) collective-permute-start(f32[264,128]{1,0:T(8,128)S(1)} %get-tuple-element.148.refs_0_), channel_id=1, source_target_pairs={{0,64},{4,68},{8,72},{12,76},{16,80},{20,84},{24,88},{28,92},{32,9... | collective-permute-start | bytes 405512 | tf_op jit(solution)/shard_map/ppermute | solution.py:305
  67.1 8.9 %collective-permute-start.19 = (f32[264,128]{1,0:T(8,128)S(1)}, f32[264,128]{1,0:T(8,128)S(1)}, u32[]{:S(2)}, u32[]{:S(2)}) collective-permute-start(f32[264,128]{1,0:T(8,128)S(1)} %get-tuple-element.148.refs_0_), channel_id=1, source_target_pairs={{0,32},{4,36},{8,40},{12,44},{16,48},{20,52},{24,56},{28,60},{32,6... | collective-permute-start | bytes 405512 | tf_op jit(solution)/shard_map/ppermute | solution.py:305
  68.7 7.2 %collective-permute-start.20 = (f32[264,128]{1,0:T(8,128)S(1)}, f32[264,128]{1,0:T(8,128)S(1)}, u32[]{:S(2)}, u32[]{:S(2)}) collective-permute-start(f32[264,128]{1,0:T(8,128)S(1)} %get-tuple-element.148.refs_0_), channel_id=1, source_target_pairs={{0,96},{4,100},{8,104},{12,108},{16,112},{20,116},{24,120},{28,124... | collective-permute-start | bytes 405512 | tf_op jit(solution)/shard_map/ppermute | solution.py:305
  76.1 7.7 %collective-permute-start.21 = (f32[264,128]{1,0:T(8,128)S(1)}, f32[264,128]{1,0:T(8,128)S(1)}, u32[]{:S(2)}, u32[]{:S(2)}) collective-permute-start(f32[264,128]{1,0:T(8,128)S(1)} %get-tuple-element.162), channel_id=1, source_target_pairs={{0,16},{4,20},{8,24},{12,28},{16,0},{20,4},{24,8},{28,12},{32,48},... | collective-permute-start | bytes 405512 | tf_op jit(solution)/shard_map/ppermute | solution.py:305
  76.9 9.2 %collective-permute-start.22 = (f32[264,128]{1,0:T(8,128)S(1)}, f32[264,128]{1,0:T(8,128)S(1)}, u32[]{:S(2)}, u32[]{:S(2)}) collective-permute-start(f32[264,128]{1,0:T(8,128)S(1)} %get-tuple-element.163), channel_id=1, source_target_pairs={{0,8},{4,12},{8,16},{12,20},{16,24},{20,28},{24,0},{28,4},{32,40},... | collective-permute-start | bytes 405512 | tf_op jit(solution)/shard_map/ppermute | solution.py:305
  78.4 7.7 %collective-permute-start.23 = (f32[264,128]{1,0:T(8,128)S(1)}, f32[264,128]{1,0:T(8,128)S(1)}, u32[]{:S(2)}, u32[]{:S(2)}) collective-permute-start(f32[264,128]{1,0:T(8,128)S(1)} %get-tuple-element.164), channel_id=1, source_target_pairs={{0,24},{4,28},{8,0},{12,4},{16,8},{20,12},{24,16},{28,20},{32,56},... | collective-permute-start | bytes 405512 | tf_op jit(solution)/shard_map/ppermute | solution.py:305
  86.2 2.4 %collective-permute-start.24 = (f32[4,264,128]{2,1,0:T(8,128)S(1)}, f32[4,264,128]{2,1,0:T(8,128)S(1)}, u32[]{:S(2)}, u32[]{:S(2)}) collective-permute-start(f32[4,264,128]{2,1,0:T(8,128)S(1)} %get-tuple-element.165), channel_id=1, source_target_pairs={{0,4},{4,0},{8,12},{12,8},{16,20},{20,16},{24,28},{28,24},{32,36},... | collective-permute-start | bytes 1622024 | tf_op jit(solution)/shard_map/ppermute | solution.py:326
